TPU v7x, 128 devices: a whole 4x4x4 slice. The times are simulated.
128 devices in a mesh: region: 4 (over y), member: 32 (over z, x, core).
Axes of the slice: x: 4, y: 4, z: 4, core: 2. Of those that a mesh axis runs over, the one named last changes fastest.
Arguments:
- member_perts: bfloat16 [256, 2, 1024, 512], P('member', None, 'region'), may hold values from -6 to 6
- alpha: float32 [256, 1024, 512], P('member', 'region'), may hold values from -0.6 to 0.6
- background: float32 [2, 1024, 512], P(None, ('region', 'member')), may hold values from -6 to 6
- obs_value: float32 [128, 112, 256], P(('region', 'member')), may hold values from -6 to 6
- obs_weight: float32 [128, 112, 256], P(('region', 'member')), may hold values from 0.5 to 8
- observed_subtile_entry: int32 [128, 112, 256], P(('region', 'member')), may hold values from 0 to 8191
- block_owner: int32 [128, 112, 1], P(('region', 'member')), may hold values from 0 to 127; in each aligned block of 112 rows (0 to 111, 112 to 223, ..., all dimensions but the last counted through in order) at most 2 rows name the same one
- block_count: int32 [128, 112], P(('region', 'member')), may hold values from 1 to 256, 25088 in all within a row
Outputs:
- gradient: float32 [256, 1024, 512], P('member', 'region')
Inputs may be any that keep to these rules, and one draw needn't show every extreme that they name: `block_owner`: no device holds more than 2 blocks of one tile owner. `block_count`: the counts of one device sum to 25088. `observed_subtile_entry`: an index into the owner's sub-tile flattened over fields, rows and columns.
All inputs are finite; a program needn't handle non-finite values.
Results may differ from a plain program's by a relative error of at most 0.0003.
Values sent between devices are 32-bit elements; how exact they have to be, the bound alone decides.
No kernel may reach another device: no remote copies, remote signals or barrier semaphores. Data moves between devices by JAX's collectives and lax.ppermute only.
A program may use at most 128 MiB of HBM per device.

v0:
```python
import math

import jax
import jax.numpy as jnp
from jax import lax
from jax.sharding import PartitionSpec as P

CAP = 2
HALF = 31


length_scale = 16.0


def padded(value, sides, width):
    for axis, dim in sides:
        devices, length = (lax.axis_size(axis), value.shape[dim])
        up = [(i, (i + 1) % devices) for i in range(devices - 1)]
        down = [(j, i) for i, j in up]
        last = lax.slice_in_dim(value, length - width, length, axis=dim)
        first = lax.slice_in_dim(value, 0, width, axis=dim)
        before = lax.ppermute(last, axis, up)
        after = lax.ppermute(first, axis, down)
        value = jnp.concatenate([before, value, after], axis=dim)
    return value


def band_weights(offsets):
    whole_range = jnp.arange(-HALF, HALF + 1).astype(jnp.float32)
    raw = jnp.exp(-whole_range * whole_range / (2.0 * length_scale * length_scale))
    norm_factor = jnp.sqrt(jnp.sum(raw * raw))
    kernel = jnp.exp(-offsets * offsets / (2.0 * length_scale * length_scale)) / norm_factor
    return jnp.where(jnp.abs(offsets) <= HALF, kernel, 0.0)


def across_columns(fields):
    field_count = fields.shape[0]
    row_count = fields.shape[1]
    col_count = fields.shape[2]
    width = 128
    blocks = col_count // width
    source = lax.broadcasted_iota(jnp.int32, (width, width), 0)
    target = lax.broadcasted_iota(jnp.int32, (width, width), 1)
    offset = (source - target).astype(jnp.float32)
    middle_rows = band_weights(offset)
    reshaped_values = fields.reshape(field_count, row_count, blocks, width)
    overall_total = jnp.einsum(
        "ykua,an->ykun", reshaped_values, middle_rows, precision=lax.Precision.HIGHEST
    )
    left_neighbour_rows = band_weights(offset - width)
    right_neighbour_rows = band_weights(offset + width)
    from_prev = jnp.einsum(
        "ykua,an->ykun",
        reshaped_values[:, :, :-1],
        left_neighbour_rows,
        precision=lax.Precision.HIGHEST,
    )
    from_next = jnp.einsum(
        "ykua,an->ykun",
        reshaped_values[:, :, 1:],
        right_neighbour_rows,
        precision=lax.Precision.HIGHEST,
    )
    zero_block = jnp.zeros((field_count, row_count, 1, width), jnp.float32)
    overall_total = (
        overall_total
        + jnp.concatenate([zero_block, from_prev], axis=2)
        + jnp.concatenate([from_next, zero_block], axis=2)
    )
    return overall_total.reshape(field_count, row_count, col_count)


def localize(fields):
    row_count = fields.shape[1]
    across_done = across_columns(fields)
    extended = padded(across_done, (("region", 1),), HALF)
    out_row = lax.broadcasted_iota(jnp.int32, (row_count, row_count + 2 * HALF), 0)
    ext_row = lax.broadcasted_iota(jnp.int32, (row_count, row_count + 2 * HALF), 1)
    vertical = band_weights((ext_row - out_row - HALF).astype(jnp.float32))
    return jnp.einsum("ye,mez->myz", vertical, extended, precision=lax.Precision.HIGHEST)


def owner_slots(target, capacity, groups):
    count = target.shape[0]
    matches = (target[:, None] == jnp.arange(groups)[None, :]).astype(jnp.float32)
    lower = (
        lax.broadcasted_iota(jnp.int32, (count, count), 1)
        < lax.broadcasted_iota(jnp.int32, (count, count), 0)
    ).astype(jnp.float32)
    earlier = jnp.dot(lower, matches, precision=lax.Precision.HIGHEST)
    position = jnp.sum(earlier * matches, axis=1).astype(jnp.int32)
    return target * capacity + position


def place_rows(slots, slot_total, values, weights, cells):
    placing = (
        lax.broadcasted_iota(jnp.int32, (slot_total, slots.shape[0]), 0) == slots[None, :]
    ).astype(jnp.float32)
    send_values = jnp.dot(placing, values, precision=lax.Precision.HIGHEST)
    send_weights = jnp.dot(placing, weights, precision=lax.Precision.HIGHEST)
    send_cells = jnp.dot(
        placing, cells.astype(jnp.float32), precision=lax.Precision.HIGHEST
    ).astype(jnp.int32)
    return (send_values, send_weights, send_cells)


def flat_misfit_pass(flat_table, flat_cells, weights, values):
    cells_line = flat_cells.reshape(-1)
    picked = flat_table[cells_line]
    misfit = weights.reshape(-1) * (picked - values.reshape(-1))
    return jnp.zeros(flat_table.shape, jnp.float32).at[cells_line].add(misfit)


def body(
    member_perts,
    alpha,
    background,
    obs_value,
    obs_weight,
    observed_subtile_entry,
    block_owner,
    block_count,
):
    members = alpha.shape[0]
    columns = alpha.shape[2]
    field_count = background.shape[0]
    sub_rows = background.shape[1]
    regions = lax.axis_size("region")
    peer_count = lax.axis_size("member")
    ens_scale = 1.0 / math.sqrt(members * peer_count - 1)
    block_size = obs_value.shape[2]
    spread = localize(alpha)
    target = block_owner[0, :, 0]
    filled = jnp.arange(block_size)[None, :] < block_count[0][:, None]
    weights = jnp.where(filled, obs_weight[0], 0.0)
    values = obs_value[0]
    cell_index = observed_subtile_entry[0]
    member_block = member_perts
    term = ens_scale * jnp.sum(member_block.astype(jnp.float32) * spread[:, None], axis=0)
    increment = lax.psum_scatter(
        jnp.transpose(term, (1, 0, 2)), "member", scatter_dimension=0, tiled=True
    )
    state_sub = background + jnp.transpose(increment, (1, 0, 2))
    devices = regions * peer_count
    slot_total = devices * CAP
    slots = owner_slots(target, CAP, devices)
    send_values, send_weights, send_cells = place_rows(
        slots, slot_total, values, weights, cell_index
    )
    got_values, got_weights, got_cells = (
        lax.all_to_all(send_values, ("region", "member"), split_axis=0, concat_axis=0, tiled=True),
        lax.all_to_all(send_weights, ("region", "member"), split_axis=0, concat_axis=0, tiled=True),
        lax.all_to_all(send_cells, ("region", "member"), split_axis=0, concat_axis=0, tiled=True),
    )
    adjoint_flat = flat_misfit_pass(state_sub.reshape(-1), got_cells, got_weights, got_values)
    adjoint = adjoint_flat.reshape(field_count, sub_rows, columns)
    member_block = member_perts
    combined = jnp.sum(
        member_block.astype(jnp.float32)
        * lax.all_gather(adjoint, "member", axis=1, tiled=True)[None],
        axis=1,
    )
    gradient = alpha + ens_scale * localize(combined)
    return gradient


def solution(mesh):
    placed = (
        P("member", None, "region", None),
        P("member", "region", None),
        P(None, ("region", "member"), None),
        P(("region", "member"), None, None),
        P(("region", "member"), None, None),
        P(("region", "member"), None, None),
        P(("region", "member"), None, None),
        P(("region", "member"), None),
    )
    return jax.shard_map(
        body, mesh=mesh, in_specs=placed, out_specs=P("member", "region", None), check_vma=False
    )
```

profile of v0, /device:TPU:1, one launch (start us, length us, event | category | flops | bytes accessed | tf_op | source)
XLA Modules:
  0.0 1083.7 jit_solution(3731880017414318355)
XLA Ops:
  10.3 11.5 %all-to-all-start = ((s32[128,2,256]{2,1,0:T(2,128)}), s32[128,2,256]{2,1,0:T(2,128)S(1)}, u32[]{:S(2)}, u32[]{:S(2)}) async-start(s32[128,2,256]{2,1,0:T(2,128)} %all_to_all.14), calls=%async_computation | async-start | bytes 524288 | tf_op jit(solution)/shard_map/all_to_all | solution.py:153
  23.1 5.3 copy.53
  28.5 5.0 fusion.28
  33.4 3.0 fusion.31
  37.7 5.6 fusion.14
  43.3 5.4 copy.41
  48.7 9.8 all-to-all-start.2
  58.5 1.3 fusion.161
  59.8 3.3 collective-permute-start
  63.1 1.8 collective-permute-start.1
  66.6 2.8 all-to-all-done.2
  69.4 8.2 all-to-all-start.1
  78.1 10.4 all-to-all-done.1
  88.7 13.4 %fusion.23 = f32[8,256,512]{1,2,0:T(8,128)} fusion(f32[8,31,512]{2,1,0:T(8,128)S(1)} %collective-permute-done.1, f32[8,256,512]{2,1,0:T(8,128)} %copy.41, f32[8,31,512]{2,1,0:T(8,128)S(1)} %collective-permute-done, f32[]{:T(128)S(6)} %sqrt.2), kind=kOutput, calls=%fused_computation.28 | convolution fusion | flops 4004785152 | bytes 9404420 | tf_op jit(solution)/shard_map/ye,mez->myz/dot_general | solution.py:80
  102.1 5.4 copy.44
  107.5 4.5 fusion
  113.2 72.4 %reduce-scatter.2.cloned.1.call-done = f32[8,2,512]{2,0,1:T(8,128)} async-done(((f32[256,2,512]{2,0,1:T(8,128)}), f32[8,2,512]{2,0,1:T(8,128)}) %reduce-scatter.2.cloned.1.call-update) | async-done | bytes 32784 | tf_op jit(solution)/shard_map/reduce_scatter | solution.py:140
  186.4 362.7 %gather_fusion = f32[65536]{0:T(1024)S(1)} fusion(f32[8192]{0:T(1024)S(1)} %bitcast.69, s32[65536]{0:T(1024)S(1)} %broadcast_clamp_fusion), kind=kCustom, calls=%fused_computation | custom fusion | bytes 786432 | tf_op jit(solution)/shard_map/gather | solution.py:109
  549.2 412.1 %scatter_custom_fusion = f32[8192]{0:T(1024)S(1)} fusion(s32[65536]{0:T(1024)S(1)} %bitcast.79, f32[65536]{0:T(1024)S(1)} %subtract_multiply_fusion, f32[]{:T(128)} %constant.10.clone.1), kind=kCustom, calls=%fused_computation.130 | custom fusion | flops 65536 | bytes 32772 | tf_op jit(solution)/shard_map/scatter-add | solution.py:111
  961.9 44.4 %all-gather.2.cloned.1.call-done = f32[2,256,512]{2,1,0:T(8,128)} async-done(((f32[2,8,512]{2,1,0:T(8,128)}), f32[2,256,512]{2,1,0:T(8,128)}) %all-gather.2.cloned.1.call-update) | async-done | bytes 1048592 | tf_op jit(solution)/shard_map/all_gather | solution.py:160
  1006.3 5.9 fusion.1
  1012.3 5.4 copy.46
  1017.6 5.1 fusion.79
  1022.8 4.2 fusion.76
  1027.0 5.5 pad_add_fusion
  1032.5 5.4 copy.50
  1039.2 3.1 collective-permute-start.2
  1042.3 1.5 collective-permute-start.3
  1043.9 9.5 collective-permute-done.2
  1053.4 3.8 collective-permute-done.3
  1057.2 14.0 %bitcast_add_fusion = f32[8,256,512]{1,2,0:T(8,128)} fusion(f32[8,256,512]{1,2,0:T(8,128)} %copy.53, f32[8,31,512]{2,1,0:T(8,128)S(1)} %collective-permute-done.3, f32[8,256,512]{2,1,0:T(8,128)} %copy.50, f32[8,31,512]{2,1,0:T(8,128)S(1)} %collective-permute-done.2, f32[]{:T(128)S(6)} %sqrt.2), kind=kOutput, calls=%fused_computation.18 | convolution fusion | flops 4006882304 | bytes 13598724 | tf_op jit(solution)/shard_map/ye,mez->myz/dot_general | solution.py:80
  1071.3 5.3 copy.54
  (42 shorter events, 11.9 us)
Async XLA Ops:
  6.5 29.9 %copy-start = (f32[1,112,256]{2,1,0:T(8,128)S(1)}, f32[1,112,256]{2,1,0:T(8,128)}, u32[]{:S(2)}) copy-start(f32[1,112,256]{2,1,0:T(8,128)} %param.11) | copy-start | bytes 344068
  10.3 38.4 %all-to-all-start = ((s32[128,2,256]{2,1,0:T(2,128)}), s32[128,2,256]{2,1,0:T(2,128)S(1)}, u32[]{:S(2)}, u32[]{:S(2)}) async-start(s32[128,2,256]{2,1,0:T(2,128)} %all_to_all.14), calls=%async_computation | async-start | bytes 524288 | tf_op jit(solution)/shard_map/all_to_all | solution.py:153
  28.4 5.0 copy-start.2
  43.3 21.6 %copy-start.4 = (f32[1,112,256]{2,1,0:T(8,128)S(1)}, f32[1,112,256]{2,1,0:T(8,128)}, u32[]{:S(2)}) copy-start(f32[1,112,256]{2,1,0:T(8,128)} %param.12) | copy-start | bytes 344068
  43.3 21.6 %copy-start.6 = (s32[1,112]{1,0:T(1,128)S(1)}, s32[1,112]{1,0:T(1,128)}, u32[]{:S(2)}) copy-start(s32[1,112]{1,0:T(1,128)} %param.15) | copy-start | bytes 1348
  48.7 20.7 %all-to-all-start.2 = ((f32[128,2,256]{2,1,0:T(2,128)}), f32[128,2,256]{2,1,0:T(2,128)S(1)}, u32[]{:S(2)}, u32[]{:S(2)}) async-start(f32[128,2,256]{2,1,0:T(2,128)} %copy.45), calls=%async_computation.3 | async-start | bytes 524288 | tf_op jit(solution)/shard_map/all_to_all | solution.py:151
  59.8 28.9 %collective-permute-start = (f32[8,31,512]{2,1,0:T(8,128)S(1)}, f32[8,31,512]{2,1,0:T(8,128)S(1)}, u32[]{:S(2)}, u32[]{:S(2)}) collective-permute-start(f32[8,31,512]{2,1,0:T(8,128)S(1)} %get-tuple-element.7), channel_id=1, source_target_pairs={{0,32},{32,64},{64,96},{1,33},{33,65},{65,97},{2,34},{34,66},{66,9... | collective-permute-start | bytes 1523720 | tf_op jit(solution)/shard_map/ppermute | solution.py:22
  63.1 25.5 %collective-permute-start.1 = (f32[8,31,512]{2,1,0:T(8,128)S(1)}, f32[8,31,512]{2,1,0:T(8,128)S(1)}, u32[]{:S(2)}, u32[]{:S(2)}) collective-permute-start(f32[8,31,512]{2,1,0:T(8,128)S(1)} %get-tuple-element.8), channel_id=1, source_target_pairs={{32,0},{64,32},{96,64},{33,1},{65,33},{97,65},{34,2},{66,34},{98,6... | collective-permute-start | bytes 1523720 | tf_op jit(solution)/shard_map/ppermute | solution.py:23
  69.4 19.2 %all-to-all-start.1 = ((f32[128,2,256]{2,1,0:T(2,128)}), f32[128,2,256]{2,1,0:T(2,128)S(1)}, u32[]{:S(2)}, u32[]{:S(2)}) async-start(f32[128,2,256]{2,1,0:T(2,128)} %copy.36), calls=%async_computation.1 | async-start | bytes 524288 | tf_op jit(solution)/shard_map/all_to_all | solution.py:152
  77.6 108.0 %reduce-scatter.2.cloned.1.call-start = ((), (), s32[]{:S(2)}) async-start(), calls=%async_computation.4 | async-start | bytes 1081344 | tf_op jit(solution)/shard_map/reduce_scatter | solution.py:140
  107.5 78.2 %copy-start.5 = (f32[2,8,512]{2,1,0:T(8,128)S(1)}, f32[2,8,512]{2,1,0:T(8,128)}, u32[]{:S(2)}) copy-start(f32[2,8,512]{2,1,0:T(8,128)} %param.10) | copy-start | bytes 98308
  113.1 893.2 %all-gather.2.cloned.1.call-start = ((), (), s32[]{:S(2)}) async-start(), calls=%async_computation.5 | async-start | bytes 1081344 | tf_op jit(solution)/shard_map/all_gather | solution.py:160
  1017.6 5.1 copy-start.3
  1039.2 14.2 %collective-permute-start.2 = (f32[8,31,512]{2,1,0:T(8,128)S(1)}, f32[8,31,512]{2,1,0:T(8,128)S(1)}, u32[]{:S(2)}, u32[]{:S(2)}) collective-permute-start(f32[8,31,512]{2,1,0:T(8,128)S(1)} %get-tuple-element.5), channel_id=1, source_target_pairs={{0,32},{32,64},{64,96},{1,33},{33,65},{65,97},{2,34},{34,66},{66,9... | collective-permute-start | bytes 1523720 | tf_op jit(solution)/shard_map/ppermute | solution.py:22
  1042.3 14.9 %collective-permute-start.3 = (f32[8,31,512]{2,1,0:T(8,128)S(1)}, f32[8,31,512]{2,1,0:T(8,128)S(1)}, u32[]{:S(2)}, u32[]{:S(2)}) collective-permute-start(f32[8,31,512]{2,1,0:T(8,128)S(1)} %get-tuple-element.6), channel_id=1, source_target_pairs={{32,0},{64,32},{96,64},{33,1},{65,33},{97,65},{34,2},{66,34},{98,6... | collective-permute-start | bytes 1523720 | tf_op jit(solution)/shard_map/ppermute | solution.py:23
  1057.2 19.4 %copy-start.1 = (f32[1,112,256]{2,1,0:T(8,128)S(1)}, f32[1,112,256]{2,1,0:T(8,128)}, u32[]{:S(2)}) copy-start(f32[1,112,256]{2,1,0:T(8,128)} %param.11) | copy-start | bytes 344068
Sparse Core Ops, SparseCore 0:
  113.3 72.3 reduce-scatter.1
  962.0 44.2 all-gather.1
where the time goes:
time: 1090 us; the launch traced here: 1080 us
  other arithmetic  426 us (39%)
  local copies, waits for them, and re-layouts  402 us (37%)
  waiting for transfers between devices  143 us (13%)
  matrix products  58.8 us (5%)
  starting transfers between devices  39.3 us (4%)
  between operations  14.6 us (1%)
    scatter-add x1, other arithmetic, flat_misfit_pass(): return jnp.zeros(flat_table.shape, jnp.float32).at[cells_line].add(misfit)  412 us
    gather x1, local copies, waits for them, and re-layouts, flat_misfit_pass(): picked = flat_table[cells_line]  363 us
    reduce_scatter x1, waiting for transfers between devices, body(): lax.psum_scatter(jnp.transpose(term, (1, 0, 2)), 'member', scatter_dimens...  72.4 us
    all_gather x1, waiting for transfers between devices, body(): lax.all_gather(adjoint, 'member', axis=1, tiled=True)[None]  44.4 us
    dot_general x2, matrix products, localize(): jnp.einsum('ye,mez->myz', vertical, extended, precision=lax.Precision.HIG...  27.5 us
  transfers between devices with their start and end apart: 9, of which 6 were waited for; matrix products, arithmetic and copies ran while one was open for 3% of the time, Pallas kernels for 0%

commit v1 on v0

v1 whole, which is shorter than its diff:
```python
import math

import jax
import jax.numpy as jnp
import ml_dtypes
import numpy as np
from jax import lax
from jax.experimental import pallas as pl
from jax.experimental.pallas import tpu as pltpu
from jax.sharding import PartitionSpec as P

HALF = 31
LENGTH_SCALE = 16.0
MEMBERS = 8
ROWS = 256
COLS = 512
EDGE = 32
SUB = 8
ENS_SCALE = 1.0 / math.sqrt(255.0)
F32 = jnp.float32
BF16 = jnp.bfloat16
PARAMS = pltpu.CompilerParams(vmem_limit_bytes=40 * 1024 * 1024)


def taps(offset):
    whole = np.arange(-HALF, HALF + 1).astype(np.float64)
    raw = np.exp(-whole * whole / (2.0 * LENGTH_SCALE**2))
    kernel = np.exp(-(offset.astype(np.float64) ** 2) / (2.0 * LENGTH_SCALE**2))
    return np.where(np.abs(offset) <= HALF, kernel / np.sqrt(np.sum(raw * raw)), 0.0)


def split_const(matrix):
    high = matrix.astype(ml_dtypes.bfloat16)
    low = (matrix - high.astype(np.float64)).astype(ml_dtypes.bfloat16)
    return np.stack([high, low])


def band(size):
    index = np.arange(size)
    return split_const(taps(index[None, :] - index[:, None]))


def edge_bands():
    index = np.arange(EDGE)
    top = taps(index[None, :] - EDGE - index[:, None])
    bottom = taps(index[None, :] + EDGE - index[:, None])
    eye = np.eye(MEMBERS)
    return (split_const(np.kron(eye, top)), split_const(np.kron(eye, bottom)))


def split(value):
    high = value.astype(BF16)
    return high, (value - high.astype(F32)).astype(BF16)


def mm(a, b):
    return jnp.dot(a, b, preferred_element_type=F32)


def conv(value, down_ref, across_ref):
    high, low = split(value)
    rows = mm(down_ref[0], high) + mm(down_ref[0], low) + mm(down_ref[1], high)
    high, low = split(rows)
    parts = []
    for block in range(2):
        k = slice(128 * block, 128 * block + 384)
        n = slice(256 * block, 256 * block + 256)
        parts.append(
            mm(high[:, k], across_ref[0, k, n])
            + mm(low[:, k], across_ref[0, k, n])
            + mm(high[:, k], across_ref[1, k, n])
        )
    return jnp.concatenate(parts, axis=1)


def whole(shape):
    return pl.BlockSpec(shape, lambda *_: (0,) * len(shape))


def cost(flops, nbytes):
    return pl.CostEstimate(flops=flops, bytes_accessed=nbytes, transcendentals=0)


def forward_body(alpha_ref, perts_ref, down_ref, across_ref, term_ref):
    spread = conv(alpha_ref[0], down_ref, across_ref)
    step = pl.program_id(0)
    for field in range(2):
        add = perts_ref[0, field].astype(F32) * spread

        @pl.when(step == 0)
        def _():
            term_ref[field] = add

        @pl.when(step > 0)
        def _():
            term_ref[field] += add


def forward(alpha, perts, down, across):
    return pl.pallas_call(
        forward_body,
        grid=(MEMBERS,),
        in_specs=[
            pl.BlockSpec((1, ROWS, COLS), lambda k: (k, 0, 0)),
            pl.BlockSpec((1, 2, ROWS, COLS), lambda k: (k, 0, 0, 0)),
            whole((2, ROWS, ROWS)),
            whole((2, COLS, COLS)),
        ],
        out_specs=whole((2, ROWS, COLS)),
        out_shape=jax.ShapeDtypeStruct((2, ROWS, COLS), F32),
        compiler_params=PARAMS,
        cost_estimate=cost(4 * 10**9, 10 * 2**20),
        name="forward_own",
    )(alpha, perts, down, across)


def forward_edge_body(
    term_ref, top_ref, bottom_ref, pt_ref, pb_ref, vt_ref, vb_ref, across_ref, mine_ref, other_ref, scr
):
    core = lax.rem(lax.axis_index("member"), 2)
    for field in range(2):
        scr[field] = term_ref[field].reshape(16, 2, SUB, COLS)
    for halo_ref, p_ref, v_ref, base in (
        (top_ref, pt_ref, vt_ref, 0),
        (bottom_ref, pb_ref, vb_ref, 14),
    ):
        spread = conv(halo_ref[...].reshape(MEMBERS * EDGE, COLS), v_ref, across_ref)
        spread = spread.reshape(MEMBERS, EDGE, COLS)
        for field in range(2):
            add = jnp.sum(p_ref[:, field].astype(F32) * spread, axis=0)
            scr[field, base : base + 2] += add.reshape(2, 2, SUB, COLS)
    for field in range(2):
        mine_ref[:, field] = scr[field, :, core]
        other_ref[:, field] = scr[field, :, 1 - core]


def forward_edge(term, top, bottom, perts, vt, vb, across):
    piece = jax.ShapeDtypeStruct((16, 2, SUB, COLS), F32)
    return pl.pallas_call(
        forward_edge_body,
        grid=(1,),
        in_specs=[
            whole((2, ROWS, COLS)),
            whole((MEMBERS, EDGE, COLS)),
            whole((MEMBERS, EDGE, COLS)),
            pl.BlockSpec((MEMBERS, 2, EDGE, COLS), lambda i: (0, 0, 0, 0)),
            pl.BlockSpec((MEMBERS, 2, EDGE, COLS), lambda i: (0, 0, ROWS // EDGE - 1, 0)),
            whole((2, 256, 256)),
            whole((2, 256, 256)),
            whole((2, COLS, COLS)),
        ],
        out_specs=[whole((16, 2, SUB, COLS))] * 2,
        out_shape=[piece, piece],
        scratch_shapes=[pltpu.VMEM((2, 16, 2, SUB, COLS), F32)],
        compiler_params=PARAMS,
        cost_estimate=cost(10**9, 6 * 2**20),
        name="forward_edge",
    )(term, top, bottom, perts, perts, vt, vb, across)


def stage_z_body(mine_ref, got_ref, *outs):
    z = lax.axis_index("member") // 8
    for step in range(4):
        at = pl.ds(lax.rem(z + step, 4) * 4, 4)
        outs[step][...] = mine_ref[at] + got_ref[at]


def stage_z(mine, got):
    piece = jax.ShapeDtypeStruct((4, 2, SUB, COLS), F32)
    return pl.pallas_call(
        stage_z_body, out_shape=[piece] * 4, compiler_params=PARAMS,
        cost_estimate=cost(10**6, 2**20), name="stage_z",
    )(mine, got)


def stage_x_body(keep_ref, a_ref, b_ref, c_ref, *outs):
    x = lax.rem(lax.axis_index("member") // 2, 4)
    for step in range(4):
        at = lax.rem(x + step, 4)
        outs[step][...] = (keep_ref[at] + a_ref[at]) + (b_ref[at] + c_ref[at])


def stage_x(keep, got):
    piece = jax.ShapeDtypeStruct((2, SUB, COLS), F32)
    return pl.pallas_call(
        stage_x_body, out_shape=[piece] * 4, compiler_params=PARAMS,
        cost_estimate=cost(10**6, 2**20), name="stage_x",
    )(keep, *got)


def adjoint_body(back_ref, keep_ref, a_ref, b_ref, c_ref, w_ref, v_ref, out_ref):
    total = (keep_ref[...] + a_ref[...]) + (b_ref[...] + c_ref[...])
    state = back_ref[...] + ENS_SCALE * total
    out_ref[...] = state * w_ref[...] - v_ref[...]


def adjoint_of(back, keep, got, w, v):
    return pl.pallas_call(
        adjoint_body, out_shape=jax.ShapeDtypeStruct((2, SUB, COLS), F32),
        compiler_params=PARAMS, cost_estimate=cost(10**5, 2**18), name="adjoint",
    )(back, keep, *got, w, v)


def gather_x_body(own_ref, a_ref, b_ref, c_ref, out_ref):
    x = lax.rem(lax.axis_index("member") // 2, 4)
    for step, ref in enumerate((own_ref, a_ref, b_ref, c_ref)):
        out_ref[lax.rem(x + 4 - step, 4)] = ref[...]


def gather_x(own, got):
    return pl.pallas_call(
        gather_x_body, out_shape=jax.ShapeDtypeStruct((4, 2, SUB, COLS), F32),
        compiler_params=PARAMS, cost_estimate=cost(10**5, 2**18), name="gather_x",
    )(own, *got)


def product_edge_body(*refs):
    mine, other = refs[0:4], refs[4:8]
    pt_ref, pb_ref, adj_ref, top_ref, bottom_ref = refs[8:]
    me = lax.axis_index("member")
    z = me // 8
    core = lax.rem(me, 2)
    for step in range(4):
        at = lax.rem(z + 4 - step, 4)
        for x in range(4):
            adj_ref[:, at, x, core] = mine[step][x]
            adj_ref[:, at, x, 1 - core] = other[step][x]
    for p_ref, out_ref, z_at, x_at in ((pt_ref, top_ref, 0, 0), (pb_ref, bottom_ref, 3, 2)):
        first = adj_ref[0, z_at, x_at : x_at + 2].reshape(EDGE, COLS)
        second = adj_ref[1, z_at, x_at : x_at + 2].reshape(EDGE, COLS)
        for k in range(MEMBERS):
            out_ref[k] = p_ref[k, 0].astype(F32) * first + p_ref[k, 1].astype(F32) * second


def product_edge(mine, other, perts):
    edge = jax.ShapeDtypeStruct((MEMBERS, EDGE, COLS), F32)
    full = (2, 4, 4, 2, SUB, COLS)
    return pl.pallas_call(
        product_edge_body,
        grid=(1,),
        in_specs=[whole((4, 2, SUB, COLS))] * 8
        + [
            pl.BlockSpec((MEMBERS, 2, EDGE, COLS), lambda i: (0, 0, 0, 0)),
            pl.BlockSpec((MEMBERS, 2, EDGE, COLS), lambda i: (0, 0, ROWS // EDGE - 1, 0)),
        ],
        out_specs=[whole(full), whole((MEMBERS, EDGE, COLS)), whole((MEMBERS, EDGE, COLS))],
        out_shape=[jax.ShapeDtypeStruct(full, F32), edge, edge],
        compiler_params=PARAMS,
        cost_estimate=cost(10**6, 4 * 2**20),
        name="product_edge",
    )(*mine, *other, perts, perts)


def backward_body(alpha_ref, perts_ref, adj_ref, down_ref, across_ref, out_ref):
    product = perts_ref[0, 0].astype(F32) * adj_ref[0] + perts_ref[0, 1].astype(F32) * adj_ref[1]
    out_ref[0] = alpha_ref[0] + ENS_SCALE * conv(product, down_ref, across_ref)


def backward(alpha, perts, adj, down, across):
    return pl.pallas_call(
        backward_body,
        grid=(MEMBERS,),
        in_specs=[
            pl.BlockSpec((1, ROWS, COLS), lambda k: (k, 0, 0)),
            pl.BlockSpec((1, 2, ROWS, COLS), lambda k: (k, 0, 0, 0)),
            whole((2, ROWS, COLS)),
            whole((2, ROWS, ROWS)),
            whole((2, COLS, COLS)),
        ],
        out_specs=pl.BlockSpec((1, ROWS, COLS), lambda k: (k, 0, 0)),
        out_shape=jax.ShapeDtypeStruct((MEMBERS, ROWS, COLS), F32),
        compiler_params=PARAMS,
        cost_estimate=cost(4 * 10**9, 14 * 2**20),
        name="backward_own",
    )(alpha, perts, adj, down, across)


def backward_edge_body(grad_ref, top_ref, bottom_ref, v_ref, across_ref, out_ref):
    def add(halo_ref):
        spread = conv(halo_ref[...].reshape(MEMBERS * EDGE, COLS), v_ref.at[0], across_ref)
        out_ref[...] = grad_ref[...] + ENS_SCALE * spread.reshape(MEMBERS, EDGE, COLS)

    @pl.when(pl.program_id(0) == 0)
    def _():
        add(top_ref)

    @pl.when(pl.program_id(0) == 1)
    def _():
        add(bottom_ref)


def backward_edge(grad, top, bottom, edges, across):
    block = pl.BlockSpec((MEMBERS, EDGE, COLS), lambda i: (0, i * (ROWS // EDGE - 1), 0))
    return pl.pallas_call(
        backward_edge_body,
        grid=(2,),
        in_specs=[
            block,
            whole((MEMBERS, EDGE, COLS)),
            whole((MEMBERS, EDGE, COLS)),
            pl.BlockSpec((1, 2, 256, 256), lambda i: (i, 0, 0, 0)),
            whole((2, COLS, COLS)),
        ],
        out_specs=block,
        out_shape=jax.ShapeDtypeStruct((MEMBERS, ROWS, COLS), F32),
        input_output_aliases={0: 0},
        compiler_params=PARAMS,
        cost_estimate=cost(10**9, 6 * 2**20),
        name="backward_edge",
    )(grad, top, bottom, edges, across)


def place_body(owner_ref, count_ref, value_ref, weight_ref, entry_ref, out_ref, used_ref):
    out_ref[...] = jnp.zeros_like(out_ref)

    def clear(i, carry):
        used_ref[i] = 0
        return carry

    lax.fori_loop(0, 128, clear, 0, unroll=8)
    lane = lax.broadcasted_iota(jnp.int32, (1, 256), 1)

    def put(b, carry):
        owner = owner_ref[b]
        slot = used_ref[owner]
        used_ref[owner] = slot + 1
        row = pl.ds(b, 1)
        weight = jnp.where(lane < count_ref[b], weight_ref[0, row, :], 0.0)
        out_ref[owner, pl.ds(slot, 1), :] = weight
        out_ref[owner, pl.ds(2 + slot, 1), :] = weight * value_ref[0, row, :]
        out_ref[owner, pl.ds(4 + slot, 1), :] = entry_ref[0, row, :].astype(F32)
        return carry

    lax.fori_loop(0, 112, put, 0, unroll=4)


def place(owner, count, value, weight, entry):
    smem = pl.BlockSpec(memory_space=pltpu.SMEM)
    vmem = pl.BlockSpec(memory_space=pltpu.VMEM)
    return pl.pallas_call(
        place_body,
        in_specs=[smem, smem, vmem, vmem, vmem],
        out_specs=vmem,
        out_shape=jax.ShapeDtypeStruct((128, 8, 256), F32),
        scratch_shapes=[pltpu.SMEM((128,), jnp.int32)],
        compiler_params=PARAMS,
        cost_estimate=cost(10**6, 2 * 2**20),
        name="place_blocks",
    )(owner, count, value, weight, entry)


SOURCES = 16


def tables_body(got_ref, w_ref, v_ref, acc):
    step = pl.program_id(0)

    @pl.when(step == 0)
    def _():
        acc[...] = jnp.zeros_like(acc)

    index = lax.broadcasted_iota(jnp.int32, (16, 512), 0).astype(F32).astype(BF16)
    one = jnp.ones((16, 512), BF16)
    zero = jnp.zeros((16, 512), BF16)

    def rows16(value):
        return jnp.broadcast_to(value, (16, 512)).astype(BF16)

    def source(s, carry):
        def line(at):
            return jnp.concatenate([got_ref[s, at : at + 1, :], got_ref[s, at + 1 : at + 2, :]], axis=1)

        weight, value, entry = line(0), line(2), line(4)
        half_row = jnp.floor(entry * (1.0 / 256.0))
        low = entry - 256.0 * half_row
        row = jnp.floor(half_row * 0.5)
        high = row + 16.0 * (half_row - 2.0 * row)
        low_at = rows16(low) - index
        high_at = rows16(high) - index
        left = []
        for quantity in (weight, value):
            first = quantity.astype(BF16).astype(F32)
            for term in (first, quantity - first):
                spread = rows16(term)
                for part in range(2):
                    left.append(jnp.where(high_at == 16.0 * part, spread, zero))
        right = [jnp.where(low_at == 16.0 * part, one, zero) for part in range(16)]
        acc[...] += lax.dot_general(
            jnp.concatenate(left, axis=0),
            jnp.concatenate(right, axis=0),
            (((1,), (1,)), ((), ())),
            preferred_element_type=F32,
        )
        return carry

    lax.fori_loop(0, SOURCES, source, 0)

    @pl.when(step == pl.num_programs(0) - 1)
    def _():
        for ref, base in ((w_ref, 0), (v_ref, 64)):
            total = acc[base : base + 32] + acc[base + 32 : base + 64]
            for field in range(2):
                at = 8 * field
                ref[field, :, 0:256] = total[at : at + 8]
                ref[field, :, 256:512] = total[16 + at : 24 + at]


def tables(got):
    piece = jax.ShapeDtypeStruct((2, SUB, COLS), F32)
    return pl.pallas_call(
        tables_body,
        grid=(128 // SOURCES,),
        in_specs=[pl.BlockSpec((SOURCES, 8, 256), lambda i: (i, 0, 0))],
        out_specs=[whole((2, SUB, COLS))] * 2,
        out_shape=[piece, piece],
        scratch_shapes=[pltpu.VMEM((128, 256), F32)],
        compiler_params=PARAMS,
        cost_estimate=cost(8 * 10**9, 2**20),
        name="weight_tables",
    )(got)


UP = [(0, 1), (1, 2), (2, 3)]
DOWN = [(1, 0), (2, 1), (3, 2)]
CORE = [(m, m ^ 1) for m in range(32)]


def along_z(step):
    return [(m, (m + 8 * step) % 32) for m in range(32)]


def along_x(step):
    return [(m, (m // 8) * 8 + ((m // 2) + step) % 4 * 2 + m % 2) for m in range(32)]


def exchange(bottom_rows, top_rows):
    return lax.ppermute(bottom_rows, "region", UP), lax.ppermute(top_rows, "region", DOWN)


def body(
    member_perts, alpha, background, obs_value, obs_weight, observed_subtile_entry, block_owner, block_count
):
    down = jnp.asarray(band(ROWS))
    across = jnp.asarray(band(COLS))
    vt, vb = [jnp.asarray(v) for v in edge_bands()]
    top, bottom = exchange(alpha[:, ROWS - EDGE :], alpha[:, :EDGE])
    send = place(block_owner[0, :, 0], block_count[0], obs_value, obs_weight, observed_subtile_entry)
    got = lax.all_to_all(send, ("region", "member"), split_axis=0, concat_axis=0, tiled=True)
    term = forward(alpha, member_perts, down, across)
    mine, other = forward_edge(term, top, bottom, member_perts, vt, vb, across)
    theirs = lax.ppermute(other, "member", CORE)
    keep, *sends = stage_z(mine, theirs)
    recv = [lax.ppermute(v, "member", along_z(s + 1)) for s, v in enumerate(sends)]
    keep, *sends = stage_x(keep, recv)
    recv = [lax.ppermute(v, "member", along_x(s + 1)) for s, v in enumerate(sends)]
    w_table, v_table = tables(got)
    adjoint = adjoint_of(background, keep, recv, w_table, v_table)
    recv = [lax.ppermute(adjoint, "member", along_x(s)) for s in (1, 2, 3)]
    line = gather_x(adjoint, recv)
    mine = [line] + [lax.ppermute(line, "member", along_z(s)) for s in (1, 2, 3)]
    other = [lax.ppermute(v, "member", CORE) for v in mine]
    adj, top_rows, bottom_rows = product_edge(mine, other, member_perts)
    top, bottom = exchange(bottom_rows, top_rows)
    grad = backward(alpha, member_perts, adj.reshape(2, ROWS, COLS), down, across)
    return backward_edge(grad, top, bottom, jnp.stack([vt, vb]), across)


def solution(mesh):
    placed = (
        P("member", None, "region", None),
        P("member", "region", None),
        P(None, ("region", "member"), None),
        P(("region", "member"), None, None),
        P(("region", "member"), None, None),
        P(("region", "member"), None, None),
        P(("region", "member"), None, None),
        P(("region", "member"), None),
    )
    return jax.shard_map(
        body, mesh=mesh, in_specs=placed, out_specs=P("member", "region", None), check_vma=False
    )
```

time: 1090 us -> 132 us (0.12)
  other arithmetic: 426 us -> 0 us
  local copies, waits for them, and re-layouts: 402 us -> 10.8 us
  waiting for transfers between devices: 143 us -> 16.5 us
  matrix products: 58.8 us -> 0 us
  Pallas kernels: 0 us -> 55.7 us
  between operations: 14.6 us -> 0.24 us
    scatter-add x1 -> x0, other arithmetic: 412 us -> none  [flat_misfit_pass(): return jnp.zeros(flat_table.shape, jnp.float32).at[cells_line].add(misfit)]
    gather x1 -> x0, local copies, waits for them, and re-layouts: 363 us -> none  [flat_misfit_pass(): picked = flat_table[cells_line]]
    reduce_scatter x1 -> x0, waiting for transfers between devices: 72.4 us -> none  [body(): lax.psum_scatter(jnp.transpose(term, (1, 0, 2)), 'member', scatter_dimens...]
    pallas_call x0 -> x11, Pallas kernels: none -> 55.7 us  [the longest x1 30.1 us: tables(): pl.pallas_call(tables_body, grid=(128 // SOURCES,), in_specs=[pl.BlockSpe...]
    dot_general x11 -> x0, matrix products: 53.3 us -> none  [the longest x2 27.5 us: localize(): jnp.einsum('ye,mez->myz', vertical, extended, precision=lax.Precision.HIG...]
    all_gather x1 -> x0, waiting for transfers between devices: 44.4 us -> none  [body(): lax.all_gather(adjoint, 'member', axis=1, tiled=True)[None]]
    ppermute x4 -> x21, starting transfers between devices: 9.73 us -> 37.2 us  [the longest x4 10.9 us: body(): other = [lax.ppermute(v, 'member', CORE) for v in mine]]
    all_to_all x3 -> x1, starting transfers between devices: 29.5 us -> 11.4 us  [body(): lax.all_to_all(send, ('region', 'member'), split_axis=0, concat_axis=0, t...]
  transfers between devices with their start and end apart: 9 -> 22, of which waited for: 6 -> 9; matrix products, arithmetic and copies ran while one was open for 3% -> 0% of each run, Pallas kernels for 0% -> 39%
where the time goes in v1:
time: 132 us
  Pallas kernels  55.7 us (42%)
  starting transfers between devices  48.6 us (37%)
  waiting for transfers between devices  16.5 us (12%)
  local copies, waits for them, and re-layouts  10.8 us (8%)
    pallas_call x1, Pallas kernels, tables(): pl.pallas_call(tables_body, grid=(128 // SOURCES,), in_specs=[pl.BlockSpe...  30.1 us
    all_to_all x1, starting transfers between devices, body(): lax.all_to_all(send, ('region', 'member'), split_axis=0, concat_axis=0, t...  11.4 us
    ppermute x4, starting transfers between devices, body(): other = [lax.ppermute(v, 'member', CORE) for v in mine]  10.9 us
    pallas_call x1, Pallas kernels, backward(): pl.pallas_call(backward_body, grid=(MEMBERS,), in_specs=[pl.BlockSpec((1,...  8.56 us
    unnamed x32, local copies, waits for them, and re-layouts  8.41 us
    pallas_call x1, Pallas kernels, forward(): pl.pallas_call(forward_body, grid=(MEMBERS,), in_specs=[pl.BlockSpec((1,...  8.21 us
    ppermute x2, starting transfers between devices, exchange(): lax.ppermute(bottom_rows, 'region', UP)  7.88 us
    ppermute x3, waiting for transfers between devices, body(): lax.ppermute(v, 'member', along_z(s + 1))  5.15 us
  transfers between devices with their start and end apart: 22, of which 9 were waited for; matrix products, arithmetic and copies ran while one was open for 0% of the time, Pallas kernels for 39%

profile of v1, /device:TPU:1, one launch (start us, length us, event | category | flops | bytes accessed | tf_op | source)
XLA Modules:
  0.0 131.8 jit_solution(1589640785273782468)
XLA Ops:
  0.0 2.4 %fusion = (f32[8,32,512]{2,1,0:T(8,128)}, f32[8,32,512]{2,1,0:T(8,128)}) fusion(f32[8,256,512]{2,1,0:T(8,128)} %alpha_ref.3), kind=kLoop, calls=%fused_computation | loop fusion | bytes 2097152 | tf_op jit(solution)/shard_map/slice | solution.py:446
  2.4 1.3 collective-permute-start.1
  3.7 4.7 %collective-permute-start = (f32[8,32,512]{2,1,0:T(8,128)}, f32[8,32,512]{2,1,0:T(8,128)S(1)}, u32[]{:S(2)}, u32[]{:S(2)}) collective-permute-start(f32[8,32,512]{2,1,0:T(8,128)} %get-tuple-element.36), channel_id=1, source_target_pairs={{0,32},{32,64},{64,96},{1,33},{33,65},{65,97},{2,34},{34,66},{66,9... | collective-permute-start | bytes 1572872 | tf_op jit(solution)/shard_map/ppermute | solution.py:437
  12.4 2.9 %place_blocks.1 = f32[128,8,256]{2,1,0:T(8,128)} custom-call(s32[112]{0:T(128)S(1)} %bitcast.4, s32[112]{0:T(128)S(1)} %bitcast.5, f32[1,112,256]{2,1,0:T(8,128)S(1)} %copy-done.10, f32[1,112,256]{2,1,0:T(8,128)S(1)} %copy-done.11, s32[1,112,256]{2,1,0:T(8,128)S(1)} %copy-done.12), custom_call_target="tpu_custom_call" | custom-call | flops 1000000 | bytes 2097152 | tf_op jit(solution)/shard_map/place_blocks/pallas_call | solution.py:340
  15.3 11.4 %all-to-all-start = ((f32[128,8,256]{2,1,0:T(8,128)}), f32[128,8,256]{2,1,0:T(8,128)S(1)}, u32[]{:S(2)}, u32[]{:S(2)}) async-start(f32[128,8,256]{2,1,0:T(8,128)} %place_blocks.1), calls=%async_computation | async-start | bytes 2097152 | tf_op jit(solution)/shard_map/all_to_all | solution.py:448
  26.8 2.2 %copy-done = bf16[8,2,256,512]{3,2,1,0:T(8,128)(2,1)S(1)} copy-done((bf16[8,2,256,512]{3,2,1,0:T(8,128)(2,1)S(1)}, bf16[8,2,256,512]{3,2,1,0:T(8,128)(2,1)}, u32[]{:S(2)}) %copy-start) | copy-done | bytes 4194328
  28.9 2.2 %copy-done.4 = f32[8,256,512]{2,1,0:T(8,128)S(1)} copy-done((f32[8,256,512]{2,1,0:T(8,128)S(1)}, f32[8,256,512]{2,1,0:T(8,128)}, u32[]{:S(2)}) %copy-start.4) | copy-done | bytes 4194328
  31.1 8.2 %forward_own.1.term_ref = f32[2,256,512]{2,1,0:T(8,128)S(1)} custom-call(f32[8,256,512]{2,1,0:T(8,128)S(1)} %copy-done.4, bf16[8,2,256,512]{3,2,1,0:T(8,128)(2,1)S(1)} %copy-done, bf16[2,256,256]{2,1,0:T(8,128)(2,1)S(1)} %copy-done.7, bf16[2,512,512]{2,1,0:T(8,128)(2,1)S(1)} %copy-done.3), custom_call_target="tpu_custom_call" | custom-call | flops 4000000000 | bytes 10485760 | tf_op jit(solution)/shard_map/forward_own/pallas_call | solution.py:100
  39.4 1.8 %forward_edge.1 = (f32[16,2,8,512]{3,2,1,0:T(8,128)S(1)}, f32[16,2,8,512]{3,2,1,0:T(8,128)S(1)}) custom-call(f32[2,256,512]{2,1,0:T(8,128)S(1)} %forward_own.1.term_ref, f32[8,32,512]{2,1,0:T(8,128)S(1)} %collective-permute-done.top_ref, f32[8,32,512]{2,1,0:T(8,128)S(1)} %collective-permute-done.1.bottom_ref, bf16[8,2,256,512]{3,2,1,0:T(8,128)(2,1)S(1)} %copy-done.1, ...), custom_call_target="tpu_custom_call" | custom-call | flops 1000000000 | bytes 6291456 | tf_op jit(solution)/shard_map/forward_edge/pallas_call | solution.py:139
  41.2 1.1 collective-permute-start.2
  42.3 1.5 %collective-permute-done.2.got_ref = f32[16,2,8,512]{3,2,1,0:T(8,128)S(1)} collective-permute-done((f32[16,2,8,512]{3,2,1,0:T(8,128)S(1)}, f32[16,2,8,512]{3,2,1,0:T(8,128)S(1)}, u32[]{:S(2)}, u32[]{:S(2)}) %collective-permute-start.2) | collective-permute-done | bytes 524320 | tf_op jit(solution)/shard_map/ppermute | solution.py:451
  44.8 2.9 %collective-permute-start.4 = (f32[4,2,8,512]{3,2,1,0:T(8,128)S(1)}, f32[4,2,8,512]{3,2,1,0:T(8,128)S(1)}, u32[]{:S(2)}, u32[]{:S(2)}) collective-permute-start(f32[4,2,8,512]{3,2,1,0:T(8,128)S(1)} %get-tuple-element.24), channel_id=1, source_target_pairs={{0,16},{1,17},{2,18},{3,19},{4,20},{5,21},{6,22},{7,23},{8,24},{9,... | collective-permute-start | bytes 393224 | tf_op jit(solution)/shard_map/ppermute | solution.py:453
  48.7 1.3 collective-permute-done.3.a_ref
  49.9 3.9 %collective-permute-done.4.b_ref = f32[4,2,8,512]{3,2,1,0:T(8,128)S(1)} collective-permute-done((f32[4,2,8,512]{3,2,1,0:T(8,128)S(1)}, f32[4,2,8,512]{3,2,1,0:T(8,128)S(1)}, u32[]{:S(2)}, u32[]{:S(2)}) %collective-permute-start.4) | collective-permute-done | bytes 131104 | tf_op jit(solution)/shard_map/ppermute | solution.py:453
  53.9 1.3 collective-permute-start.6
  55.1 2.4 %collective-permute-start.7 = (f32[2,8,512]{2,1,0:T(8,128)S(1)}, f32[2,8,512]{2,1,0:T(8,128)S(1)}, u32[]{:S(2)}, u32[]{:S(2)}) collective-permute-start(f32[2,8,512]{2,1,0:T(8,128)S(1)} %get-tuple-element.28), channel_id=1, source_target_pairs={{0,4},{1,5},{2,6},{3,7},{4,0},{5,1},{6,2},{7,3},{8,12},{9,13},{10,... | collective-permute-start | bytes 98312 | tf_op jit(solution)/shard_map/ppermute | solution.py:455
  57.6 1.2 collective-permute-start.8
  58.7 30.1 %weight_tables.1 = (f32[2,8,512]{2,1,0:T(8,128)S(1)}, f32[2,8,512]{2,1,0:T(8,128)S(1)}) custom-call(f32[128,8,256]{2,1,0:T(8,128)S(1)} %all-to-all-done.got_ref), custom_call_target="tpu_custom_call" | custom-call | flops 8000000000 | bytes 1048576 | tf_op jit(solution)/shard_map/weight_tables/pallas_call | solution.py:410
  89.0 2.1 %collective-permute-start.10 = (f32[2,8,512]{2,1,0:T(8,128)S(1)}, f32[2,8,512]{2,1,0:T(8,128)S(1)}, u32[]{:S(2)}, u32[]{:S(2)}) collective-permute-start(f32[2,8,512]{2,1,0:T(8,128)S(1)} %adjoint.1.own_ref), channel_id=1, source_target_pairs={{0,4},{1,5},{2,6},{3,7},{4,0},{5,1},{6,2},{7,3},{8,12},{9,13},{10,... | collective-permute-start | bytes 98312 | tf_op jit(solution)/shard_map/ppermute | solution.py:458
  91.8 1.6 %collective-permute-done.10.b_ref = f32[2,8,512]{2,1,0:T(8,128)S(1)} collective-permute-done((f32[2,8,512]{2,1,0:T(8,128)S(1)}, f32[2,8,512]{2,1,0:T(8,128)S(1)}, u32[]{:S(2)}, u32[]{:S(2)}) %collective-permute-start.10) | collective-permute-done | bytes 32800 | tf_op jit(solution)/shard_map/ppermute | solution.py:458
  93.4 1.7 %collective-permute-done.9.a_ref = f32[2,8,512]{2,1,0:T(8,128)S(1)} collective-permute-done((f32[2,8,512]{2,1,0:T(8,128)S(1)}, f32[2,8,512]{2,1,0:T(8,128)S(1)}, u32[]{:S(2)}, u32[]{:S(2)}) %collective-permute-start.9) | collective-permute-done | bytes 32800 | tf_op jit(solution)/shard_map/ppermute | solution.py:458
  95.1 2.1 %collective-permute-start.14 = (f32[4,2,8,512]{3,2,1,0:T(8,128)S(1)}, f32[4,2,8,512]{3,2,1,0:T(8,128)S(1)}, u32[]{:S(2)}, u32[]{:S(2)}) collective-permute-start(f32[4,2,8,512]{3,2,1,0:T(8,128)S(1)} %gather_x.1.refs_0_), channel_id=1, source_target_pairs={{0,24},{1,25},{2,26},{3,27},{4,28},{5,29},{6,30},{7,31},{8,0},{9,1... | collective-permute-start | bytes 393224 | tf_op jit(solution)/shard_map/ppermute | solution.py:460
  98.0 4.7 %collective-permute-start.15 = (f32[4,2,8,512]{3,2,1,0:T(8,128)S(1)}, f32[4,2,8,512]{3,2,1,0:T(8,128)S(1)}, u32[]{:S(2)}, u32[]{:S(2)}) collective-permute-start(f32[4,2,8,512]{3,2,1,0:T(8,128)S(1)} %gather_x.1.refs_0_), channel_id=1, source_target_pairs={{0,1},{1,0},{2,3},{3,2},{4,5},{5,4},{6,7},{7,6},{8,9},{9,8},{10,11... | collective-permute-start | bytes 393224 | tf_op jit(solution)/shard_map/ppermute | solution.py:461
  102.7 2.2 %collective-permute-start.18 = (f32[4,2,8,512]{3,2,1,0:T(8,128)S(1)}, f32[4,2,8,512]{3,2,1,0:T(8,128)S(1)}, u32[]{:S(2)}, u32[]{:S(2)}) collective-permute-start(f32[4,2,8,512]{3,2,1,0:T(8,128)S(1)} %collective-permute-done.14.refs_3_), channel_id=1, source_target_pairs={{0,1},{1,0},{2,3},{3,2},{4,5},{5,4},{6,7},{7,6},{8,9},{9,8},{10,11... | collective-permute-start | bytes 393224 | tf_op jit(solution)/shard_map/ppermute | solution.py:461
  105.0 2.6 %collective-permute-start.17 = (f32[4,2,8,512]{3,2,1,0:T(8,128)S(1)}, f32[4,2,8,512]{3,2,1,0:T(8,128)S(1)}, u32[]{:S(2)}, u32[]{:S(2)}) collective-permute-start(f32[4,2,8,512]{3,2,1,0:T(8,128)S(1)} %collective-permute-done.13.refs_2_), channel_id=1, source_target_pairs={{0,1},{1,0},{2,3},{3,2},{4,5},{5,4},{6,7},{7,6},{8,9},{9,8},{10,11... | collective-permute-start | bytes 393224 | tf_op jit(solution)/shard_map/ppermute | solution.py:461
  107.6 1.3 %collective-permute-start.16 = (f32[4,2,8,512]{3,2,1,0:T(8,128)S(1)}, f32[4,2,8,512]{3,2,1,0:T(8,128)S(1)}, u32[]{:S(2)}, u32[]{:S(2)}) collective-permute-start(f32[4,2,8,512]{3,2,1,0:T(8,128)S(1)} %collective-permute-done.12.refs_1_), channel_id=1, source_target_pairs={{0,1},{1,0},{2,3},{3,2},{4,5},{5,4},{6,7},{7,6},{8,9},{9,8},{10,11... | collective-permute-start | bytes 393224 | tf_op jit(solution)/shard_map/ppermute | solution.py:461
  110.2 3.2 %collective-permute-start.19 = (f32[8,32,512]{2,1,0:T(8,128)S(1)}, f32[8,32,512]{2,1,0:T(8,128)S(1)}, u32[]{:S(2)}, u32[]{:S(2)}) collective-permute-start(f32[8,32,512]{2,1,0:T(8,128)S(1)} %get-tuple-element.33), channel_id=1, source_target_pairs={{0,32},{32,64},{64,96},{1,33},{33,65},{65,97},{2,34},{34,66},{66,9... | collective-permute-start | bytes 1572872 | tf_op jit(solution)/shard_map/ppermute | solution.py:437
  113.4 1.3 collective-permute-start.20
  114.7 8.6 %backward_own.1.grad_ref = f32[8,256,512]{2,1,0:T(8,128)} custom-call(f32[8,256,512]{2,1,0:T(8,128)S(1)} %copy-done.5, bf16[8,2,256,512]{3,2,1,0:T(8,128)(2,1)S(1)} %copy-done.2, f32[2,256,512]{2,1,0:T(8,128)S(1)} %bitcast.3, bf16[2,256,256]{2,1,0:T(8,128)(2,1)S(1)} %copy-done.7, bf16[2,512,512]{2,1,0:T(8,128)(2,1)S(1)} %copy-done.3), custom_call_target="tpu_custom_call" | custom-call | flops 4000000000 | bytes 14680064 | tf_op jit(solution)/shard_map/backward_own/pallas_call | solution.py:260
  123.3 1.0 collective-permute-done.19.top_ref
  124.3 3.8 %collective-permute-done.20.bottom_ref = f32[8,32,512]{2,1,0:T(8,128)S(1)} collective-permute-done((f32[8,32,512]{2,1,0:T(8,128)S(1)}, f32[8,32,512]{2,1,0:T(8,128)S(1)}, u32[]{:S(2)}, u32[]{:S(2)}) %collective-permute-start.20) | collective-permute-done | bytes 524320 | tf_op jit(solution)/shard_map/ppermute | solution.py:437
  128.1 3.6 %backward_edge.1 = f32[8,256,512]{2,1,0:T(8,128)} custom-call(f32[8,256,512]{2,1,0:T(8,128)} %backward_own.1.grad_ref, f32[8,32,512]{2,1,0:T(8,128)S(1)} %collective-permute-done.19.top_ref, f32[8,32,512]{2,1,0:T(8,128)S(1)} %collective-permute-done.20.bottom_ref, bf16[2,2,256,256]{3,2,1,0:T(8,128)(2,1)S(1)} %copy-done.6, ...), custom_call_target="tpu_custom_call", output_to_operand_aliasing={{}: (0, {})} | custom-call | flops 1000000000 | bytes 6291456 | tf_op jit(solution)/shard_map/backward_edge/pallas_call | solution.py:294
  (56 shorter events, 8.9 us)
Async XLA Ops:
  0.0 26.7 %copy-start.3 = (bf16[2,512,512]{2,1,0:T(8,128)(2,1)S(1)}, bf16[2,512,512]{2,1,0:T(8,128)(2,1)}, u32[]{:S(2)}) copy-start(bf16[2,512,512]{2,1,0:T(8,128)(2,1)} %constant.9.clone.across_ref) | copy-start | bytes 3145732
  0.0 26.7 %copy-start.7 = (bf16[2,256,256]{2,1,0:T(8,128)(2,1)S(1)}, bf16[2,256,256]{2,1,0:T(8,128)(2,1)}, u32[]{:S(2)}) copy-start(bf16[2,256,256]{2,1,0:T(8,128)(2,1)} %constant.8.clone.down_ref) | copy-start | bytes 786436
  2.4 37.0 %collective-permute-start.1 = (f32[8,32,512]{2,1,0:T(8,128)}, f32[8,32,512]{2,1,0:T(8,128)S(1)}, u32[]{:S(2)}, u32[]{:S(2)}) collective-permute-start(f32[8,32,512]{2,1,0:T(8,128)} %get-tuple-element.35), channel_id=1, source_target_pairs={{32,0},{64,32},{96,64},{33,1},{65,33},{97,65},{34,2},{66,34},{98,6... | collective-permute-start | bytes 1572872 | tf_op jit(solution)/shard_map/ppermute | solution.py:437
  3.7 35.7 %collective-permute-start = (f32[8,32,512]{2,1,0:T(8,128)}, f32[8,32,512]{2,1,0:T(8,128)S(1)}, u32[]{:S(2)}, u32[]{:S(2)}) collective-permute-start(f32[8,32,512]{2,1,0:T(8,128)} %get-tuple-element.36), channel_id=1, source_target_pairs={{0,32},{32,64},{64,96},{1,33},{33,65},{65,97},{2,34},{34,66},{66,9... | collective-permute-start | bytes 1572872 | tf_op jit(solution)/shard_map/ppermute | solution.py:437
  15.3 43.4 %all-to-all-start = ((f32[128,8,256]{2,1,0:T(8,128)}), f32[128,8,256]{2,1,0:T(8,128)S(1)}, u32[]{:S(2)}, u32[]{:S(2)}) async-start(f32[128,8,256]{2,1,0:T(8,128)} %place_blocks.1), calls=%async_computation | async-start | bytes 2097152 | tf_op jit(solution)/shard_map/all_to_all | solution.py:448
  26.7 2.2 %copy-start = (bf16[8,2,256,512]{3,2,1,0:T(8,128)(2,1)S(1)}, bf16[8,2,256,512]{3,2,1,0:T(8,128)(2,1)}, u32[]{:S(2)}) copy-start(bf16[8,2,256,512]{3,2,1,0:T(8,128)(2,1)} %perts_ref.3) | copy-start | bytes 12582916
  31.1 8.2 %copy-start.1 = (bf16[8,2,256,512]{3,2,1,0:T(8,128)(2,1)S(1)}, bf16[8,2,256,512]{3,2,1,0:T(8,128)(2,1)}, u32[]{:S(2)}) copy-start(bf16[8,2,256,512]{3,2,1,0:T(8,128)(2,1)} %perts_ref.3) | copy-start | bytes 12582916
  31.1 8.3 %copy-start.8 = (bf16[2,256,256]{2,1,0:T(8,128)(2,1)S(1)}, bf16[2,256,256]{2,1,0:T(8,128)(2,1)}, u32[]{:S(2)}) copy-start(bf16[2,256,256]{2,1,0:T(8,128)(2,1)} %constant.11.clone.vb_ref) | copy-start | bytes 786436
  31.1 8.3 %copy-start.9 = (bf16[2,256,256]{2,1,0:T(8,128)(2,1)S(1)}, bf16[2,256,256]{2,1,0:T(8,128)(2,1)}, u32[]{:S(2)}) copy-start(bf16[2,256,256]{2,1,0:T(8,128)(2,1)} %constant.10.clone.vt_ref) | copy-start | bytes 786436
  41.2 2.7 %collective-permute-start.2 = (f32[16,2,8,512]{3,2,1,0:T(8,128)S(1)}, f32[16,2,8,512]{3,2,1,0:T(8,128)S(1)}, u32[]{:S(2)}, u32[]{:S(2)}) collective-permute-start(f32[16,2,8,512]{3,2,1,0:T(8,128)S(1)} %get-tuple-element.21), channel_id=1, source_target_pairs={{0,1},{1,0},{2,3},{3,2},{4,5},{5,4},{6,7},{7,6},{8,9},{9,8},{10,11... | collective-permute-start | bytes 1572872 | tf_op jit(solution)/shard_map/ppermute | solution.py:451
  43.9 6.0 %collective-permute-start.3 = (f32[4,2,8,512]{3,2,1,0:T(8,128)S(1)}, f32[4,2,8,512]{3,2,1,0:T(8,128)S(1)}, u32[]{:S(2)}, u32[]{:S(2)}) collective-permute-start(f32[4,2,8,512]{3,2,1,0:T(8,128)S(1)} %get-tuple-element.23), channel_id=1, source_target_pairs={{0,8},{1,9},{2,10},{3,11},{4,12},{5,13},{6,14},{7,15},{8,16},{9,17... | collective-permute-start | bytes 393224 | tf_op jit(solution)/shard_map/ppermute | solution.py:453
  44.8 9.0 %collective-permute-start.4 = (f32[4,2,8,512]{3,2,1,0:T(8,128)S(1)}, f32[4,2,8,512]{3,2,1,0:T(8,128)S(1)}, u32[]{:S(2)}, u32[]{:S(2)}) collective-permute-start(f32[4,2,8,512]{3,2,1,0:T(8,128)S(1)} %get-tuple-element.24), channel_id=1, source_target_pairs={{0,16},{1,17},{2,18},{3,19},{4,20},{5,21},{6,22},{7,23},{8,24},{9,... | collective-permute-start | bytes 393224 | tf_op jit(solution)/shard_map/ppermute | solution.py:453
  47.8 6.1 %collective-permute-start.5 = (f32[4,2,8,512]{3,2,1,0:T(8,128)S(1)}, f32[4,2,8,512]{3,2,1,0:T(8,128)S(1)}, u32[]{:S(2)}, u32[]{:S(2)}) collective-permute-start(f32[4,2,8,512]{3,2,1,0:T(8,128)S(1)} %get-tuple-element.25), channel_id=1, source_target_pairs={{0,24},{1,25},{2,26},{3,27},{4,28},{5,29},{6,30},{7,31},{8,0},{9,1... | collective-permute-start | bytes 393224 | tf_op jit(solution)/shard_map/ppermute | solution.py:453
  53.9 35.0 %collective-permute-start.6 = (f32[2,8,512]{2,1,0:T(8,128)S(1)}, f32[2,8,512]{2,1,0:T(8,128)S(1)}, u32[]{:S(2)}, u32[]{:S(2)}) collective-permute-start(f32[2,8,512]{2,1,0:T(8,128)S(1)} %get-tuple-element.27), channel_id=1, source_target_pairs={{0,2},{1,3},{2,4},{3,5},{4,6},{5,7},{6,0},{7,1},{8,10},{9,11},{10,... | collective-permute-start | bytes 98312 | tf_op jit(solution)/shard_map/ppermute | solution.py:455
  55.1 33.8 %collective-permute-start.7 = (f32[2,8,512]{2,1,0:T(8,128)S(1)}, f32[2,8,512]{2,1,0:T(8,128)S(1)}, u32[]{:S(2)}, u32[]{:S(2)}) collective-permute-start(f32[2,8,512]{2,1,0:T(8,128)S(1)} %get-tuple-element.28), channel_id=1, source_target_pairs={{0,4},{1,5},{2,6},{3,7},{4,0},{5,1},{6,2},{7,3},{8,12},{9,13},{10,... | collective-permute-start | bytes 98312 | tf_op jit(solution)/shard_map/ppermute | solution.py:455
  57.6 31.3 %copy-start.13 = (f32[2,8,512]{2,1,0:T(8,128)S(1)}, f32[2,8,512]{2,1,0:T(8,128)}, u32[]{:S(2)}) copy-start(f32[2,8,512]{2,1,0:T(8,128)} %back_ref.1) | copy-start | bytes 98308
  57.6 31.3 %collective-permute-start.8 = (f32[2,8,512]{2,1,0:T(8,128)S(1)}, f32[2,8,512]{2,1,0:T(8,128)S(1)}, u32[]{:S(2)}, u32[]{:S(2)}) collective-permute-start(f32[2,8,512]{2,1,0:T(8,128)S(1)} %get-tuple-element.29), channel_id=1, source_target_pairs={{0,6},{1,7},{2,0},{3,1},{4,2},{5,3},{6,4},{7,5},{8,14},{9,15},{10,... | collective-permute-start | bytes 98312 | tf_op jit(solution)/shard_map/ppermute | solution.py:455
  58.7 51.2 %copy-start.2 = (bf16[8,2,256,512]{3,2,1,0:T(8,128)(2,1)S(1)}, bf16[8,2,256,512]{3,2,1,0:T(8,128)(2,1)}, u32[]{:S(2)}) copy-start(bf16[8,2,256,512]{3,2,1,0:T(8,128)(2,1)} %perts_ref.3) | copy-start | bytes 12582916
  88.9 2.8 %collective-permute-start.11 = (f32[2,8,512]{2,1,0:T(8,128)S(1)}, f32[2,8,512]{2,1,0:T(8,128)S(1)}, u32[]{:S(2)}, u32[]{:S(2)}) collective-permute-start(f32[2,8,512]{2,1,0:T(8,128)S(1)} %adjoint.1.own_ref), channel_id=1, source_target_pairs={{0,6},{1,7},{2,0},{3,1},{4,2},{5,3},{6,4},{7,5},{8,14},{9,15},{10,... | collective-permute-start | bytes 98312 | tf_op jit(solution)/shard_map/ppermute | solution.py:458
  89.0 4.3 %collective-permute-start.10 = (f32[2,8,512]{2,1,0:T(8,128)S(1)}, f32[2,8,512]{2,1,0:T(8,128)S(1)}, u32[]{:S(2)}, u32[]{:S(2)}) collective-permute-start(f32[2,8,512]{2,1,0:T(8,128)S(1)} %adjoint.1.own_ref), channel_id=1, source_target_pairs={{0,4},{1,5},{2,6},{3,7},{4,0},{5,1},{6,2},{7,3},{8,12},{9,13},{10,... | collective-permute-start | bytes 98312 | tf_op jit(solution)/shard_map/ppermute | solution.py:458
  91.1 4.0 %collective-permute-start.9 = (f32[2,8,512]{2,1,0:T(8,128)S(1)}, f32[2,8,512]{2,1,0:T(8,128)S(1)}, u32[]{:S(2)}, u32[]{:S(2)}) collective-permute-start(f32[2,8,512]{2,1,0:T(8,128)S(1)} %adjoint.1.own_ref), channel_id=1, source_target_pairs={{0,2},{1,3},{2,4},{3,5},{4,6},{5,7},{6,0},{7,1},{8,10},{9,11},{10,... | collective-permute-start | bytes 98312 | tf_op jit(solution)/shard_map/ppermute | solution.py:458
  95.1 19.6 %copy-start.5 = (f32[8,256,512]{2,1,0:T(8,128)S(1)}, f32[8,256,512]{2,1,0:T(8,128)}, u32[]{:S(2)}) copy-start(f32[8,256,512]{2,1,0:T(8,128)} %alpha_ref.3) | copy-start | bytes 12582916
  95.1 7.7 %collective-permute-start.14 = (f32[4,2,8,512]{3,2,1,0:T(8,128)S(1)}, f32[4,2,8,512]{3,2,1,0:T(8,128)S(1)}, u32[]{:S(2)}, u32[]{:S(2)}) collective-permute-start(f32[4,2,8,512]{3,2,1,0:T(8,128)S(1)} %gather_x.1.refs_0_), channel_id=1, source_target_pairs={{0,24},{1,25},{2,26},{3,27},{4,28},{5,29},{6,30},{7,31},{8,0},{9,1... | collective-permute-start | bytes 393224 | tf_op jit(solution)/shard_map/ppermute | solution.py:460
  97.2 7.7 %collective-permute-start.13 = (f32[4,2,8,512]{3,2,1,0:T(8,128)S(1)}, f32[4,2,8,512]{3,2,1,0:T(8,128)S(1)}, u32[]{:S(2)}, u32[]{:S(2)}) collective-permute-start(f32[4,2,8,512]{3,2,1,0:T(8,128)S(1)} %gather_x.1.refs_0_), channel_id=1, source_target_pairs={{0,16},{1,17},{2,18},{3,19},{4,20},{5,21},{6,22},{7,23},{8,24},{9,... | collective-permute-start | bytes 393224 | tf_op jit(solution)/shard_map/ppermute | solution.py:460
  98.0 9.5 %collective-permute-start.12 = (f32[4,2,8,512]{3,2,1,0:T(8,128)S(1)}, f32[4,2,8,512]{3,2,1,0:T(8,128)S(1)}, u32[]{:S(2)}, u32[]{:S(2)}) collective-permute-start(f32[4,2,8,512]{3,2,1,0:T(8,128)S(1)} %gather_x.1.refs_0_), channel_id=1, source_target_pairs={{0,8},{1,9},{2,10},{3,11},{4,12},{5,13},{6,14},{7,15},{8,16},{9,17... | collective-permute-start | bytes 393224 | tf_op jit(solution)/shard_map/ppermute | solution.py:460
  98.0 10.9 %collective-permute-start.15 = (f32[4,2,8,512]{3,2,1,0:T(8,128)S(1)}, f32[4,2,8,512]{3,2,1,0:T(8,128)S(1)}, u32[]{:S(2)}, u32[]{:S(2)}) collective-permute-start(f32[4,2,8,512]{3,2,1,0:T(8,128)S(1)} %gather_x.1.refs_0_), channel_id=1, source_target_pairs={{0,1},{1,0},{2,3},{3,2},{4,5},{5,4},{6,7},{7,6},{8,9},{9,8},{10,11... | collective-permute-start | bytes 393224 | tf_op jit(solution)/shard_map/ppermute | solution.py:461
  102.7 6.2 %collective-permute-start.18 = (f32[4,2,8,512]{3,2,1,0:T(8,128)S(1)}, f32[4,2,8,512]{3,2,1,0:T(8,128)S(1)}, u32[]{:S(2)}, u32[]{:S(2)}) collective-permute-start(f32[4,2,8,512]{3,2,1,0:T(8,128)S(1)} %collective-permute-done.14.refs_3_), channel_id=1, source_target_pairs={{0,1},{1,0},{2,3},{3,2},{4,5},{5,4},{6,7},{7,6},{8,9},{9,8},{10,11... | collective-permute-start | bytes 393224 | tf_op jit(solution)/shard_map/ppermute | solution.py:461
  105.0 4.0 %collective-permute-start.17 = (f32[4,2,8,512]{3,2,1,0:T(8,128)S(1)}, f32[4,2,8,512]{3,2,1,0:T(8,128)S(1)}, u32[]{:S(2)}, u32[]{:S(2)}) collective-permute-start(f32[4,2,8,512]{3,2,1,0:T(8,128)S(1)} %collective-permute-done.13.refs_2_), channel_id=1, source_target_pairs={{0,1},{1,0},{2,3},{3,2},{4,5},{5,4},{6,7},{7,6},{8,9},{9,8},{10,11... | collective-permute-start | bytes 393224 | tf_op jit(solution)/shard_map/ppermute | solution.py:461
  107.6 2.3 %collective-permute-start.16 = (f32[4,2,8,512]{3,2,1,0:T(8,128)S(1)}, f32[4,2,8,512]{3,2,1,0:T(8,128)S(1)}, u32[]{:S(2)}, u32[]{:S(2)}) collective-permute-start(f32[4,2,8,512]{3,2,1,0:T(8,128)S(1)} %collective-permute-done.12.refs_1_), channel_id=1, source_target_pairs={{0,1},{1,0},{2,3},{3,2},{4,5},{5,4},{6,7},{7,6},{8,9},{9,8},{10,11... | collective-permute-start | bytes 393224 | tf_op jit(solution)/shard_map/ppermute | solution.py:461
  110.2 14.1 %collective-permute-start.19 = (f32[8,32,512]{2,1,0:T(8,128)S(1)}, f32[8,32,512]{2,1,0:T(8,128)S(1)}, u32[]{:S(2)}, u32[]{:S(2)}) collective-permute-start(f32[8,32,512]{2,1,0:T(8,128)S(1)} %get-tuple-element.33), channel_id=1, source_target_pairs={{0,32},{32,64},{64,96},{1,33},{33,65},{65,97},{2,34},{34,66},{66,9... | collective-permute-start | bytes 1572872 | tf_op jit(solution)/shard_map/ppermute | solution.py:437
  113.4 14.7 %collective-permute-start.20 = (f32[8,32,512]{2,1,0:T(8,128)S(1)}, f32[8,32,512]{2,1,0:T(8,128)S(1)}, u32[]{:S(2)}, u32[]{:S(2)}) collective-permute-start(f32[8,32,512]{2,1,0:T(8,128)S(1)} %get-tuple-element.34), channel_id=1, source_target_pairs={{32,0},{64,32},{96,64},{33,1},{65,33},{97,65},{34,2},{66,34},{98,6... | collective-permute-start | bytes 1572872 | tf_op jit(solution)/shard_map/ppermute | solution.py:437
  114.7 13.4 %copy-start.6 = (bf16[2,2,256,256]{3,2,1,0:T(8,128)(2,1)S(1)}, bf16[2,2,256,256]{3,2,1,0:T(8,128)(2,1)}, u32[]{:S(2)}) copy-start(bf16[2,2,256,256]{3,2,1,0:T(8,128)(2,1)} %constant.22.v_ref) | copy-start | bytes 1572868
  (6 other events, 6.2 us)

commit v2 on v0

v2 whole, which is shorter than its diff:
```python
import math

import jax
import jax.numpy as jnp
import ml_dtypes
import numpy as np
from jax import lax
from jax.experimental import pallas as pl
from jax.experimental.pallas import tpu as pltpu
from jax.sharding import PartitionSpec as P

HALF = 31
LENGTH_SCALE = 16.0
MEMBERS = 8
ROWS = 256
COLS = 512
EDGE = 32
SUB = 8
ENS_SCALE = 1.0 / math.sqrt(255.0)
F32 = jnp.float32
BF16 = jnp.bfloat16
PARAMS = pltpu.CompilerParams(vmem_limit_bytes=28 * 1024 * 1024)
STREAM = pltpu.CompilerParams(vmem_limit_bytes=58 * 1024 * 1024)
FORWARD = pltpu.CompilerParams(vmem_limit_bytes=52 * 1024 * 1024)
BACKWARD = pltpu.CompilerParams(vmem_limit_bytes=51 * 1024 * 1024)


def taps(offset):
    whole = np.arange(-HALF, HALF + 1).astype(np.float64)
    raw = np.exp(-whole * whole / (2.0 * LENGTH_SCALE**2))
    kernel = np.exp(-(offset.astype(np.float64) ** 2) / (2.0 * LENGTH_SCALE**2))
    return np.where(np.abs(offset) <= HALF, kernel / np.sqrt(np.sum(raw * raw)), 0.0)


def split_const(matrix):
    high = matrix.astype(ml_dtypes.bfloat16)
    low = (matrix - high.astype(np.float64)).astype(ml_dtypes.bfloat16)
    return high, low


def stack_terms(high, low, axis):
    return np.concatenate([high, high, low], axis=axis)


def band(size):
    index = np.arange(size)
    return taps(index[None, :] - index[:, None])


def constants():
    index = np.arange(EDGE)
    eye = np.eye(MEMBERS)
    top = np.kron(eye, taps(index[None, :] - EDGE - index[:, None]))
    bottom = np.kron(eye, taps(index[None, :] + EDGE - index[:, None]))
    downs = [stack_terms(*split_const(v), 1) for v in (band(ROWS), top, bottom)]
    wide = band(COLS)
    blocks = [wide[128 * i : 128 * i + 384, 256 * i : 256 * i + 256] for i in range(2)]
    across = np.stack([stack_terms(*split_const(v), 0) for v in blocks])
    return jnp.asarray(downs[0]), jnp.asarray(np.stack(downs[1:])), jnp.asarray(across)


def split(value):
    high = value.astype(BF16)
    return high, (value - high.astype(F32)).astype(BF16)


def mm(a, b):
    return jnp.dot(a, b, preferred_element_type=F32)


def terms(value, axis):
    high, low = split(value)
    return jnp.concatenate([high, low, high], axis=axis)


def down_rows(values, downs):
    return jnp.concatenate([mm(down, terms(value, 0)) for value, down in zip(values, downs)], axis=0)


def across_columns(rows, across_ref):
    high, low = split(rows)
    parts = []
    for block in range(2):
        k = slice(128 * block, 128 * block + 384)
        parts.append(mm(jnp.concatenate([high[:, k], low[:, k], high[:, k]], axis=1), across_ref[block]))
    return jnp.concatenate(parts, axis=1)


def conv(values, downs, across_ref):
    return across_columns(down_rows(values, downs), across_ref)


def whole(shape):
    return pl.BlockSpec(shape, lambda *_: (0,) * len(shape))


def cost(flops, nbytes):
    return pl.CostEstimate(flops=flops, bytes_accessed=nbytes, transcendentals=0)


VMEM = pl.BlockSpec(memory_space=pltpu.VMEM)
SMEM = pl.BlockSpec(memory_space=pltpu.SMEM)
HBM = pl.BlockSpec(memory_space=pltpu.HBM)
EDGES = (MEMBERS, EDGE, COLS)
PERTS_EDGES = (MEMBERS, 2, EDGE, COLS)
PIECES = (16, 2, SUB, COLS)


def out(shape, dtype=F32):
    return jax.ShapeDtypeStruct(shape, dtype)


def place_body(
    owner_hbm, count_hbm, value_hbm, weight_hbm, entry_hbm, alpha_hbm, perts_hbm,
    send_ref, first_ref, last_ref, perts_first_ref, perts_last_ref, owner_ref, count_ref, value_ref, weight_ref, entry_ref, used_ref, sems,
):
    pairs = [
        (owner_hbm, owner_ref), (count_hbm, count_ref),
        (value_hbm, value_ref), (weight_hbm, weight_ref), (entry_hbm, entry_ref),
        (alpha_hbm.at[:, :EDGE, :], first_ref), (alpha_hbm.at[:, ROWS - EDGE :, :], last_ref),
        (perts_hbm.at[:, :, :EDGE, :], perts_first_ref), (perts_hbm.at[:, :, ROWS - EDGE :, :], perts_last_ref),
    ]
    copies = [pltpu.make_async_copy(src, dst, sems.at[i]) for i, (src, dst) in enumerate(pairs)]
    for copy in copies:
        copy.start()
    send_ref[...] = jnp.zeros_like(send_ref)

    def clear(i, carry):
        used_ref[i] = 0
        return carry

    lax.fori_loop(0, 128, clear, 0, unroll=8)
    lane = lax.broadcasted_iota(jnp.int32, (1, 256), 1)
    for copy in copies[:5]:
        copy.wait()

    def put(b, carry):
        owner = owner_ref[b]
        slot = used_ref[owner]
        used_ref[owner] = slot + 1
        row = pl.ds(b, 1)
        weight = jnp.where(lane < count_ref[b], weight_ref[0, row, :], 0.0)
        put_at = pl.ds(slot, 1)
        send_ref[owner, put_at, 0:256] = weight
        send_ref[owner, put_at, 256:512] = weight * value_ref[0, row, :]
        send_ref[owner, put_at, 512:768] = entry_ref[0, row, :].astype(F32)
        return carry

    lax.fori_loop(0, 112, put, 0, unroll=4)
    for copy in copies[5:]:
        copy.wait()


def place(owner, count, value, weight, entry, alpha, perts):
    return pl.pallas_call(
        place_body,
        in_specs=[HBM] * 7,
        out_specs=[VMEM] * 5,
        out_shape=[
            out((128, 2, 768)), out(EDGES), out(EDGES), out(PERTS_EDGES, BF16), out(PERTS_EDGES, BF16),
        ],
        scratch_shapes=[
            pltpu.SMEM(owner.shape, jnp.int32), pltpu.SMEM(count.shape, jnp.int32),
            pltpu.VMEM(value.shape, F32), pltpu.VMEM(value.shape, F32), pltpu.VMEM(value.shape, jnp.int32),
            pltpu.SMEM((128,), jnp.int32), pltpu.SemaphoreType.DMA((9,)),
        ],
        compiler_params=STREAM,
        cost_estimate=cost(10**9, 0),
        name="place",
    )(owner, count, value, weight, entry, alpha, perts)


GROUP = 4
FIELD = (2, 16, 2, SUB, COLS)


def member_copies(source, target, sems):
    return [pltpu.make_async_copy(source.at[k], target.at[k], sems.at[k]) for k in range(MEMBERS)]


def forward_body(
    alpha_hbm, perts_hbm, down_hbm, across_hbm, term_ref,
    alpha_ref, perts_ref, down_ref, across_ref, alpha_sems, perts_sems, const_sems,
):
    alpha_copies = member_copies(alpha_hbm, alpha_ref, alpha_sems)
    perts_copies = member_copies(perts_hbm, perts_ref, perts_sems)
    down_copy = pltpu.make_async_copy(down_hbm, down_ref, const_sems.at[0])
    across_copy = pltpu.make_async_copy(across_hbm, across_ref, const_sems.at[1])
    down_copy.start()
    for base in range(0, MEMBERS, GROUP):
        for k in range(base, base + GROUP):
            alpha_copies[k].start()
        if base == 0:
            across_copy.start()
        for k in range(base, base + GROUP):
            perts_copies[k].start()
    down_copy.wait()
    rows = None
    for base in range(0, MEMBERS + GROUP, GROUP):
        before = rows
        if base < MEMBERS:
            members = range(base, base + GROUP)
            for k in members:
                alpha_copies[k].wait()
        if base == GROUP:
            across_copy.wait()
        if base > 0:
            for k in range(base - GROUP, base):
                perts_copies[k].wait()
        if base < MEMBERS:
            rows = down_rows([alpha_ref[k] for k in members], [down_ref[...]] * GROUP)
        if base > 0:
            spread = across_columns(before, across_ref)
            for field in range(2):
                total = perts_ref[base - GROUP, field].astype(F32) * spread[:ROWS]
                for m in range(1, GROUP):
                    part = spread[ROWS * m : ROWS * (m + 1)]
                    total += perts_ref[base - GROUP + m, field].astype(F32) * part
                total = total.reshape(FIELD[1:])
                if base == GROUP:
                    term_ref[field] = total
                else:
                    term_ref[field] += total


def forward(alpha, perts, down, across):
    return pl.pallas_call(
        forward_body,
        in_specs=[HBM] * 4,
        out_specs=VMEM,
        out_shape=out(FIELD),
        scratch_shapes=[
            pltpu.VMEM(alpha.shape, F32), pltpu.VMEM(perts.shape, BF16),
            pltpu.VMEM(down.shape, BF16), pltpu.VMEM(across.shape, BF16),
            pltpu.SemaphoreType.DMA((MEMBERS,)), pltpu.SemaphoreType.DMA((MEMBERS,)),
            pltpu.SemaphoreType.DMA((2,)),
        ],
        compiler_params=FORWARD,
        cost_estimate=cost(10**6, 0),
        name="forward",
    )(alpha, perts, down, across)


def forward_edge_body(
    term_ref, top_ref, bottom_ref, perts_first_ref, perts_last_ref, down_ref, across_ref, mine_ref, other_ref
):
    core = lax.rem(lax.axis_index("member"), 2)
    for field in range(2):
        mine_ref[:, field] = term_ref[field, :, core]
        other_ref[:, field] = term_ref[field, :, 1 - core]
    halo = [ref[...].reshape(MEMBERS * EDGE, COLS) for ref in (top_ref, bottom_ref)]
    spread = conv(halo, [down_ref[0], down_ref[1]], across_ref).reshape((2,) + EDGES)
    for side, p_ref in enumerate((perts_first_ref, perts_last_ref)):
        at = slice(14 * side, 14 * side + 2)
        for field in range(2):
            total = jnp.sum(p_ref[:, field].astype(F32) * spread[side], axis=0).reshape(2, 2, SUB, COLS)
            even = core == 0
            mine_ref[at, field] += jnp.where(even, total[:, 0], total[:, 1])
            other_ref[at, field] += jnp.where(even, total[:, 1], total[:, 0])


def forward_edge(term, top, bottom, perts_first, perts_last, down, across):
    return pl.pallas_call(
        forward_edge_body,
        in_specs=[VMEM] * 7,
        out_specs=[VMEM] * 2,
        out_shape=[out(PIECES), out(PIECES)],
        compiler_params=PARAMS,
        cost_estimate=cost(10**9, 6 * 2**20),
        name="forward_edge",
    )(term, top, bottom, perts_first, perts_last, down, across)


def adjoint_body(back_ref, got_ref, w_ref, v_ref, out_ref):
    state = back_ref[...] + ENS_SCALE * jnp.sum(got_ref[...], axis=0)
    out_ref[...] = jnp.broadcast_to((state * w_ref[...] - v_ref[...])[None], PIECES)


def adjoint_of(back, got, w, v):
    return pl.pallas_call(
        adjoint_body, in_specs=[VMEM] * 4, out_specs=VMEM, out_shape=out(PIECES), compiler_params=PARAMS,
        cost_estimate=cost(10**5, 2**20), name="adjoint",
    )(back, got, w, v)


def perts_edges_body(first_in_ref, last_in_ref, anchor_ref, first_ref, last_ref):
    first_ref[...] = first_in_ref[...].astype(F32)
    last_ref[...] = last_in_ref[...].astype(F32)


def perts_edges(first, last, anchor):
    return pl.pallas_call(
        perts_edges_body, in_specs=[VMEM, VMEM, HBM], out_specs=[VMEM] * 2,
        out_shape=[out(PERTS_EDGES), out(PERTS_EDGES)],
        compiler_params=PARAMS, cost_estimate=cost(10**10, 0), name="perts_edges",
    )(first, last, anchor)


def assemble_body(mine_ref, other_ref, adj_ref, first_ref, last_ref):
    core = lax.rem(lax.axis_index("member"), 2)
    for field in range(2):
        adj_ref[field, :, core] = mine_ref[:, field]
        adj_ref[field, :, 1 - core] = other_ref[:, field]
    for field in range(2):
        first_ref[field] = adj_ref[field, :2]
        last_ref[field] = adj_ref[field, 14:]


def assemble(mine, other):
    edge = out((2, 2, 2, SUB, COLS))
    return pl.pallas_call(
        assemble_body, in_specs=[VMEM] * 2, out_specs=[VMEM] * 3,
        out_shape=[out((2, 16, 2, SUB, COLS)), edge, edge], compiler_params=PARAMS,
        cost_estimate=cost(10**5, 2 * 2**20), name="assemble",
    )(mine, other)


def backward_body(
    alpha_hbm, perts_hbm, adj_ref, down_hbm, across_hbm, grad_hbm, edge_ref,
    scr, alpha_ref, perts_ref, down_ref, across_ref, alpha_sems, perts_sems, grad_sems, const_sems,
):
    alpha_copies = member_copies(alpha_hbm, alpha_ref, alpha_sems)
    perts_copies = member_copies(perts_hbm, perts_ref, perts_sems)
    copies = member_copies(scr, grad_hbm, grad_sems)
    down_copy = pltpu.make_async_copy(down_hbm, down_ref, const_sems.at[0])
    across_copy = pltpu.make_async_copy(across_hbm, across_ref, const_sems.at[1])
    down_copy.start()
    for base in range(0, MEMBERS, GROUP):
        for k in range(base, base + GROUP):
            perts_copies[k].start()
        if base == 0:
            across_copy.start()
        for k in range(base, base + GROUP):
            alpha_copies[k].start()
    down_copy.wait()
    rows = None
    for base in range(0, MEMBERS + GROUP, GROUP):
        before = rows
        if base < MEMBERS:
            for k in range(base, base + GROUP):
                perts_copies[k].wait()
        if base == GROUP:
            across_copy.wait()
        if base > 0:
            for k in range(base - GROUP, base):
                alpha_copies[k].wait()
        if base < MEMBERS:
            products = []
            for k in range(base, base + GROUP):
                product = perts_ref[k, 0].astype(F32) * adj_ref[0]
                products.append(product + perts_ref[k, 1].astype(F32) * adj_ref[1])
            rows = down_rows(products, [down_ref[...]] * GROUP)
        if base > 0:
            spread = across_columns(before, across_ref)
            for m in range(GROUP):
                k = base - GROUP + m
                scr[k] = alpha_ref[k] + ENS_SCALE * spread[ROWS * m : ROWS * (m + 1)]
                edge_ref[0, k] = scr[k, :EDGE]
                edge_ref[1, k] = scr[k, ROWS - EDGE :]
            for k in range(base - GROUP, base):
                copies[k].start()
    for copy in copies:
        copy.wait()


def backward(alpha, perts, adj, down, across):
    return pl.pallas_call(
        backward_body,
        in_specs=[HBM, HBM, VMEM, HBM, HBM],
        out_specs=[HBM, VMEM],
        out_shape=[out(alpha.shape), out((2,) + EDGES)],
        scratch_shapes=[
            pltpu.VMEM(alpha.shape, F32), pltpu.VMEM(alpha.shape, F32), pltpu.VMEM(perts.shape, BF16),
            pltpu.VMEM(down.shape, BF16), pltpu.VMEM(across.shape, BF16),
            pltpu.SemaphoreType.DMA((MEMBERS,)), pltpu.SemaphoreType.DMA((MEMBERS,)),
            pltpu.SemaphoreType.DMA((MEMBERS,)), pltpu.SemaphoreType.DMA((2,)),
        ],
        compiler_params=BACKWARD,
        cost_estimate=cost(10**6, 0),
        name="backward_own",
    )(alpha, perts, adj, down, across)


def backward_edge_body(
    grad_hbm, edge_ref, pt_ref, pb_ref, at_ref, ab_ref, down_ref, across_ref, out_hbm, scr, sems
):
    products = []
    for p_ref, a_ref in ((pt_ref, at_ref), (pb_ref, ab_ref)):
        first, second = [a_ref[field].reshape(1, EDGE, COLS) for field in range(2)]
        products.append((p_ref[:, 0] * first + p_ref[:, 1] * second).reshape(MEMBERS * EDGE, COLS))
    spread = conv(products, [down_ref[0], down_ref[1]], across_ref).reshape((2,) + EDGES)
    copies = []
    for side in range(2):
        scr[side] = edge_ref[side] + ENS_SCALE * spread[side]
        at = (ROWS - EDGE) * side
        copies.append(pltpu.make_async_copy(scr.at[side], out_hbm.at[:, at : at + EDGE, :], sems.at[side]))
        copies[side].start()
    for copy in copies:
        copy.wait()


def backward_edge(grad, edge, pt, pb, at, ab, down, across):
    return pl.pallas_call(
        backward_edge_body,
        in_specs=[HBM] + [VMEM] * 7,
        out_specs=HBM,
        out_shape=out(grad.shape),
        input_output_aliases={0: 0},
        scratch_shapes=[pltpu.VMEM((2,) + EDGES, F32), pltpu.SemaphoreType.DMA((2,))],
        compiler_params=PARAMS,
        cost_estimate=cost(10**9, 6 * 2**20),
        name="backward_edge",
    )(grad, edge, pt, pb, at, ab, down, across)


SOURCES = 16
HIGH = 64
LOW = 128


def tables_body(got_ref, w_ref, v_ref, acc):
    step = pl.program_id(0)

    @pl.when(step == 0)
    def _():
        acc[...] = jnp.zeros_like(acc)

    index = lax.broadcasted_iota(jnp.int32, (16, 512), 0).astype(F32).astype(BF16)
    one = jnp.ones((16, 512), BF16)
    zero = jnp.zeros((16, 512), BF16)

    def rows16(value):
        return jnp.broadcast_to(value, (16, 512)).astype(BF16)

    def source(s, carry):
        def line(at):
            return jnp.concatenate([got_ref[s, 0:1, at : at + 256], got_ref[s, 1:2, at : at + 256]], axis=1)

        weight, value, entry = line(0), line(256), line(512)
        chunk = jnp.floor(entry * (1.0 / LOW))
        row = jnp.floor(chunk * 0.25)
        low_at = rows16(entry - LOW * chunk) - index
        high_at = rows16(row + 16.0 * (chunk - 4.0 * row)) - index
        hits = [high_at == 16.0 * part for part in range(HIGH // 16)]
        left = []
        for quantity in (weight, value):
            first = quantity.astype(BF16).astype(F32)
            for term in (first, quantity - first):
                spread = rows16(term)
                left += [jnp.where(hit, spread, zero) for hit in hits]
        right = [jnp.where(low_at == 16.0 * part, one, zero) for part in range(LOW // 16)]
        acc[...] += lax.dot_general(
            jnp.concatenate(left, axis=0),
            jnp.concatenate(right, axis=0),
            (((1,), (1,)), ((), ())),
            preferred_element_type=F32,
        )
        return carry

    lax.fori_loop(0, SOURCES, source, 0, unroll=8)

    @pl.when(step == pl.num_programs(0) - 1)
    def _():
        for ref, base in ((w_ref, 0), (v_ref, 2 * HIGH)):
            total = acc[base : base + HIGH] + acc[base + HIGH : base + 2 * HIGH]
            for field in range(2):
                for chunk in range(4):
                    at = 16 * chunk + 8 * field
                    ref[field, :, LOW * chunk : LOW * (chunk + 1)] = total[at : at + 8]


def tables(got):
    piece = jax.ShapeDtypeStruct((2, SUB, COLS), F32)
    return pl.pallas_call(
        tables_body,
        grid=(128 // SOURCES,),
        in_specs=[pl.BlockSpec((SOURCES, 2, 768), lambda i: (i, 0, 0))],
        out_specs=[whole((2, SUB, COLS))] * 2,
        out_shape=[piece, piece],
        scratch_shapes=[pltpu.VMEM((4 * HIGH, LOW), F32)],
        compiler_params=PARAMS,
        cost_estimate=cost(12 * 10**9, 2**20),
        name="weight_tables",
    )(got)


UP = [(0, 1), (1, 2), (2, 3)]
DOWN = [(1, 0), (2, 1), (3, 2)]
CORE = [(m, m ^ 1) for m in range(32)]
SAME_CORE = [[2 * q + core for q in range(16)] for core in range(2)]


def exchange(last, first):
    return lax.ppermute(last, "region", UP), lax.ppermute(first, "region", DOWN)


def among_sixteen(pieces):
    return lax.all_to_all(
        pieces, "member", split_axis=0, concat_axis=0, axis_index_groups=SAME_CORE, tiled=True
    )


def body(
    member_perts, alpha, background, obs_value, obs_weight, observed_subtile_entry, block_owner, block_count
):
    down, edge_downs, across = constants()
    send, first, last, perts_first, perts_last = place(
        block_owner[0, :, 0], block_count[0], obs_value, obs_weight, observed_subtile_entry, alpha, member_perts
    )
    top, bottom = exchange(last, first)
    term = forward(alpha, member_perts, down, across)
    got = lax.all_to_all(send, ("region", "member"), split_axis=0, concat_axis=0, tiled=True)
    mine, other = forward_edge(term, top, bottom, perts_first, perts_last, edge_downs, across)
    pieces = among_sixteen(mine + lax.ppermute(other, "member", CORE))
    w_table, v_table = tables(got)
    adjoint = adjoint_of(background, pieces, w_table, v_table)
    mine = among_sixteen(adjoint)
    first, last = perts_edges(perts_first, perts_last, adjoint)
    perts_top, perts_bottom = exchange(last, first)
    adj, first, last = assemble(mine, lax.ppermute(mine, "member", CORE))
    adj_top, adj_bottom = exchange(last, first)
    grad, edge = backward(alpha, member_perts, adj.reshape(2, ROWS, COLS), down, across)
    return backward_edge(grad, edge, perts_top, perts_bottom, adj_top, adj_bottom, edge_downs, across)


def solution(mesh):
    placed = (
        P("member", None, "region", None),
        P("member", "region", None),
        P(None, ("region", "member"), None),
        P(("region", "member"), None, None),
        P(("region", "member"), None, None),
        P(("region", "member"), None, None),
        P(("region", "member"), None, None),
        P(("region", "member"), None),
    )
    return jax.shard_map(
        body, mesh=mesh, in_specs=placed, out_specs=P("member", "region", None), check_vma=False
    )
```

time: 1090 us -> 102 us (0.09)
  other arithmetic: 426 us -> 0.88 us
  local copies, waits for them, and re-layouts: 402 us -> 1.08 us
  waiting for transfers between devices: 143 us -> 16 us
  matrix products: 58.8 us -> 0 us
  Pallas kernels: 0 us -> 41.6 us
  between operations: 14.6 us -> 0.43 us
    scatter-add x1 -> x0, other arithmetic: 412 us -> none  [flat_misfit_pass(): return jnp.zeros(flat_table.shape, jnp.float32).at[cells_line].add(misfit)]
    gather x1 -> x0, local copies, waits for them, and re-layouts: 363 us -> none  [flat_misfit_pass(): picked = flat_table[cells_line]]
    reduce_scatter x1 -> x0, waiting for transfers between devices: 72.4 us -> none  [body(): lax.psum_scatter(jnp.transpose(term, (1, 0, 2)), 'member', scatter_dimens...]
    dot_general x11 -> x0, matrix products: 53.3 us -> none  [the longest x2 27.5 us: localize(): jnp.einsum('ye,mez->myz', vertical, extended, precision=lax.Precision.HIG...]
    all_gather x1 -> x0, waiting for transfers between devices: 44.4 us -> none  [body(): lax.all_gather(adjoint, 'member', axis=1, tiled=True)[None]]
    pallas_call x0 -> x9, Pallas kernels: none -> 41.6 us  [the longest x1 11.7 us: tables(): pl.pallas_call(tables_body, grid=(128 // SOURCES,), in_specs=[pl.BlockSpe...]
    reshape x4 -> x0, local copies, waits for them, and re-layouts: 11.7 us -> none  [the longest x2 10.7 us: across_columns(): return overall_total.reshape(field_count, row_count, col_count)]
    reduce_sum x3 -> x0, other arithmetic: 11.1 us -> none  [the longest x1 5.95 us: body(): jnp.sum(member_block.astype(jnp.float32) * lax.all_gather(adjoint, 'membe...]
  transfers between devices with their start and end apart: 9 -> 11, of which waited for: 6 -> 6; matrix products, arithmetic and copies ran while one was open for 3% -> 1% of each run, Pallas kernels for 0% -> 34%
where the time goes in v2:
time: 102 us; the launch traced here: 100 us
  Pallas kernels  41.6 us (41%)
  starting transfers between devices  40.3 us (40%)
  waiting for transfers between devices  16 us (16%)
  local copies, waits for them, and re-layouts  1.08 us (1%)
    all_to_all x2, starting transfers between devices, among_sixteen(): lax.all_to_all(pieces, 'member', split_axis=0, concat_axis=0, axis_index_...  13.6 us
    all_to_all x1, starting transfers between devices, body(): lax.all_to_all(send, ('region', 'member'), split_axis=0, concat_axis=0, t...  11.8 us
    pallas_call x1, Pallas kernels, tables(): pl.pallas_call(tables_body, grid=(128 // SOURCES,), in_specs=[pl.BlockSpe...  11.7 us
    pallas_call x1, Pallas kernels, backward(): pl.pallas_call(backward_body, in_specs=[HBM, HBM, VMEM, HBM, HBM], out_sp...  9.37 us
    pallas_call x1, Pallas kernels, forward(): pl.pallas_call(forward_body, in_specs=[HBM] * 4, out_specs=VMEM, out_shap...  8.4 us
    ppermute x3, starting transfers between devices, exchange(): lax.ppermute(last, 'region', UP)  7.49 us
    ppermute x3, waiting for transfers between devices, exchange(): lax.ppermute(first, 'region', DOWN)  5.85 us
    all_to_all x2, waiting for transfers between devices, among_sixteen(): lax.all_to_all(pieces, 'member', split_axis=0, concat_axis=0, axis_index_...  5.19 us
  transfers between devices with their start and end apart: 11, of which 6 were waited for; matrix products, arithmetic and copies ran while one was open for 1% of the time, Pallas kernels for 34%

profile of v2, /device:TPU:1, one launch (start us, length us, event | category | flops | bytes accessed | tf_op | source)
XLA Modules:
  0.0 100.2 jit_solution(15262512911194299580)
XLA Ops:
  0.0 3.6 %place.1 = (f32[128,2,768]{2,1,0:T(2,128)}, f32[8,32,512]{2,1,0:T(8,128)}, f32[8,32,512]{2,1,0:T(8,128)}, bf16[8,2,32,512]{3,2,1,0:T(8,128)(2,1)}, bf16[8,2,32,512]{3,2,1,0:T(8,128)(2,1)}) custom-call(s32[112]{0:T(128)} %bitcast.4, s32[112]{0:T(128)} %bitcast.5, f32[1,112,256]{2,1,0:T(8,128)} %value_hbm.1, f32[1,112,256]{2,1,0:T(8,128)} %weight_hbm.1, ...), custom_call_target="tpu_custom_call" | custom-call | flops 1000000000 | tf_op jit(solution)/shard_map/place/pallas_call | solution.py:155
  3.6 4.8 %collective-permute-start = (f32[8,32,512]{2,1,0:T(8,128)}, f32[8,32,512]{2,1,0:T(8,128)}, u32[]{:S(2)}, u32[]{:S(2)}) collective-permute-start(f32[8,32,512]{2,1,0:T(8,128)} %get-tuple-element.21), channel_id=1, source_target_pairs={{0,32},{32,64},{64,96},{1,33},{33,65},{65,97},{2,34},{34,66},{66,9... | collective-permute-start | bytes 1572872 | tf_op jit(solution)/shard_map/ppermute | solution.py:494
  8.4 1.3 %collective-permute-start.1 = (f32[8,32,512]{2,1,0:T(8,128)}, f32[8,32,512]{2,1,0:T(8,128)}, u32[]{:S(2)}, u32[]{:S(2)}) collective-permute-start(f32[8,32,512]{2,1,0:T(8,128)} %get-tuple-element.22), channel_id=1, source_target_pairs={{32,0},{64,32},{96,64},{33,1},{65,33},{97,65},{34,2},{66,34},{98,6... | collective-permute-start | bytes 1572872 | tf_op jit(solution)/shard_map/ppermute | solution.py:494
  9.7 11.8 %all-to-all-start.1 = ((f32[128,2,768]{2,1,0:T(2,128)}), f32[128,2,768]{2,1,0:T(2,128)S(1)}, u32[]{:S(2)}, u32[]{:S(2)}) async-start(f32[128,2,768]{2,1,0:T(2,128)} %get-tuple-element.27), calls=%async_computation.1 | async-start | bytes 1572864 | tf_op jit(solution)/shard_map/all_to_all | solution.py:512
  21.6 0.0 copy-start
  21.6 0.0 copy-start.2
  21.6 8.4 %forward.1.term_ref = f32[2,16,2,8,512]{4,3,2,1,0:T(8,128)S(1)} custom-call(f32[8,256,512]{2,1,0:T(8,128)} %alpha_hbm.5, bf16[8,2,256,512]{3,2,1,0:T(8,128)(2,1)} %perts_hbm.5, bf16[256,768]{1,0:T(8,128)(2,1)S(1)} %copy-done.3, bf16[2,1152,256]{2,1,0:T(8,128)(2,1)} %constant.8.clone.across_hbm.across_ref), custom_call_target="tpu_custom_call" | custom-call | flops 1000000 | tf_op jit(solution)/shard_map/forward/pallas_call | solution.py:227
  30.1 2.6 %forward_edge.1 = (f32[16,2,8,512]{3,2,1,0:T(8,128)S(1)}, f32[16,2,8,512]{3,2,1,0:T(8,128)S(1)}) custom-call(f32[2,16,2,8,512]{4,3,2,1,0:T(8,128)S(1)} %forward.1.term_ref, f32[8,32,512]{2,1,0:T(8,128)} %collective-permute-done.top_ref, f32[8,32,512]{2,1,0:T(8,128)} %collective-permute-done.1.bottom_ref, bf16[8,2,32,512]{3,2,1,0:T(8,128)(2,1)S(1)} %copy-done.4, ...), custom_call_target="tpu_custom_call" | custom-call | flops 1000000000 | bytes 6291456 | tf_op jit(solution)/shard_map/forward_edge/pallas_call | solution.py:263
  32.7 1.1 %collective-permute-start.2 = (f32[16,2,8,512]{3,2,1,0:T(8,128)S(1)}, f32[16,2,8,512]{3,2,1,0:T(8,128)S(1)}, u32[]{:S(2)}, u32[]{:S(2)}) collective-permute-start(f32[16,2,8,512]{3,2,1,0:T(8,128)S(1)} %get-tuple-element.26), channel_id=1, source_target_pairs={{0,1},{1,0},{2,3},{3,2},{4,5},{5,4},{6,7},{7,6},{8,9},{9,8},{10,11... | collective-permute-start | bytes 1572872 | tf_op jit(solution)/shard_map/ppermute | solution.py:514
  33.9 1.5 %collective-permute-done.2 = f32[16,2,8,512]{3,2,1,0:T(8,128)S(1)} collective-permute-done((f32[16,2,8,512]{3,2,1,0:T(8,128)S(1)}, f32[16,2,8,512]{3,2,1,0:T(8,128)S(1)}, u32[]{:S(2)}, u32[]{:S(2)}) %collective-permute-start.2) | collective-permute-done | bytes 524320 | tf_op jit(solution)/shard_map/ppermute | solution.py:514
  35.4 0.9 add.3
  36.3 1.9 %all-to-all-done.1.got_ref = f32[128,2,768]{2,1,0:T(2,128)S(1)} async-done(((f32[128,2,768]{2,1,0:T(2,128)}), f32[128,2,768]{2,1,0:T(2,128)S(1)}, u32[]{:S(2)}, u32[]{:S(2)}) %all-to-all-start.1) | async-done | bytes 786464 | tf_op jit(solution)/shard_map/all_to_all | solution.py:512
  38.1 6.9 %all-to-all-start = ((f32[16,2,8,512]{3,2,1,0:T(8,128)}), f32[16,2,8,512]{3,2,1,0:T(8,128)S(1)}, u32[]{:S(2)}, u32[]{:S(2)}) async-start(f32[16,2,8,512]{3,2,1,0:T(8,128)} %add.3), calls=%async_computation | async-start | bytes 1048576 | tf_op jit(solution)/shard_map/all_to_all | solution.py:498
  45.1 0.0 copy-start.8
  45.1 11.7 %weight_tables.1 = (f32[2,8,512]{2,1,0:T(8,128)S(1)}, f32[2,8,512]{2,1,0:T(8,128)S(1)}) custom-call(f32[128,2,768]{2,1,0:T(2,128)S(1)} %all-to-all-done.1.got_ref), custom_call_target="tpu_custom_call" | custom-call | flops 12000000000 | bytes 1048576 | tf_op jit(solution)/shard_map/weight_tables/pallas_call | solution.py:474
  56.9 0.9 adjoint.1.anchor_ref
  57.7 6.6 %all-to-all-start.2 = ((f32[16,2,8,512]{3,2,1,0:T(8,128)}), f32[16,2,8,512]{3,2,1,0:T(8,128)S(1)}, u32[]{:S(2)}, u32[]{:S(2)}) async-start(f32[16,2,8,512]{3,2,1,0:T(8,128)} %adjoint.1.anchor_ref), calls=%async_computation.2 | async-start | bytes 1048576 | tf_op jit(solution)/shard_map/all_to_all | solution.py:498
  64.4 1.0 %copy-done.7 = bf16[8,2,32,512]{3,2,1,0:T(8,128)(2,1)S(1)} copy-done((bf16[8,2,32,512]{3,2,1,0:T(8,128)(2,1)S(1)}, bf16[8,2,32,512]{3,2,1,0:T(8,128)(2,1)}, u32[]{:S(2)}) %copy-start.7) | copy-done | bytes 524312
  65.4 1.4 %perts_edges.1 = (f32[8,2,32,512]{3,2,1,0:T(8,128)}, f32[8,2,32,512]{3,2,1,0:T(8,128)}) custom-call(bf16[8,2,32,512]{3,2,1,0:T(8,128)(2,1)S(1)} %copy-done.5, bf16[8,2,32,512]{3,2,1,0:T(8,128)(2,1)S(1)} %copy-done.7, f32[16,2,8,512]{3,2,1,0:T(8,128)} %adjoint.1.anchor_ref), custom_call_target="tpu_custom_call" | custom-call | flops 10000000000 | tf_op jit(solution)/shard_map/perts_edges/pallas_call | solution.py:292
  66.9 1.3 %collective-permute-start.4 = (f32[8,2,32,512]{3,2,1,0:T(8,128)}, f32[8,2,32,512]{3,2,1,0:T(8,128)S(1)}, u32[]{:S(2)}, u32[]{:S(2)}) collective-permute-start(f32[8,2,32,512]{3,2,1,0:T(8,128)} %get-tuple-element.33), channel_id=1, source_target_pairs={{0,32},{32,64},{64,96},{1,33},{33,65},{65,97},{2,34},{34,66},{66,9... | collective-permute-start | bytes 3145736 | tf_op jit(solution)/shard_map/ppermute | solution.py:494
  68.2 1.3 %collective-permute-start.5 = (f32[8,2,32,512]{3,2,1,0:T(8,128)}, f32[8,2,32,512]{3,2,1,0:T(8,128)}, u32[]{:S(2)}, u32[]{:S(2)}) collective-permute-start(f32[8,2,32,512]{3,2,1,0:T(8,128)} %get-tuple-element.34), channel_id=1, source_target_pairs={{32,0},{64,32},{96,64},{33,1},{65,33},{97,65},{34,2},{66,34},{98,6... | collective-permute-start | bytes 3145736 | tf_op jit(solution)/shard_map/ppermute | solution.py:494
  69.5 5.2 %all-to-all-done.2.mine_ref = f32[16,2,8,512]{3,2,1,0:T(8,128)S(1)} async-done(((f32[16,2,8,512]{3,2,1,0:T(8,128)}), f32[16,2,8,512]{3,2,1,0:T(8,128)S(1)}, u32[]{:S(2)}, u32[]{:S(2)}) %all-to-all-start.2) | async-done | bytes 524320 | tf_op jit(solution)/shard_map/all_to_all | solution.py:498
  74.7 2.2 %collective-permute-start.3 = (f32[16,2,8,512]{3,2,1,0:T(8,128)S(1)}, f32[16,2,8,512]{3,2,1,0:T(8,128)S(1)}, u32[]{:S(2)}, u32[]{:S(2)}) collective-permute-start(f32[16,2,8,512]{3,2,1,0:T(8,128)S(1)} %all-to-all-done.2.mine_ref), channel_id=1, source_target_pairs={{0,1},{1,0},{2,3},{3,2},{4,5},{5,4},{6,7},{7,6},{8,9},{9,8},{10,11... | collective-permute-start | bytes 1572872 | tf_op jit(solution)/shard_map/ppermute | solution.py:520
  76.9 1.5 %collective-permute-done.3.other_ref = f32[16,2,8,512]{3,2,1,0:T(8,128)S(1)} collective-permute-done((f32[16,2,8,512]{3,2,1,0:T(8,128)S(1)}, f32[16,2,8,512]{3,2,1,0:T(8,128)S(1)}, u32[]{:S(2)}, u32[]{:S(2)}) %collective-permute-start.3) | collective-permute-done | bytes 524320 | tf_op jit(solution)/shard_map/ppermute | solution.py:520
  78.4 0.1 assemble.1
  78.5 1.3 %collective-permute-start.6 = (f32[2,2,2,8,512]{4,3,2,1,0:T(8,128)S(1)}, f32[2,2,2,8,512]{4,3,2,1,0:T(8,128)S(1)}, u32[]{:S(2)}, u32[]{:S(2)}) collective-permute-start(f32[2,2,2,8,512]{4,3,2,1,0:T(8,128)S(1)} %get-tuple-element.35), channel_id=1, source_target_pairs={{0,32},{32,64},{64,96},{1,33},{33,65},{65,97},{2,34},{34,66},{66,9... | collective-permute-start | bytes 393224 | tf_op jit(solution)/shard_map/ppermute | solution.py:494
  79.8 1.5 %collective-permute-start.7 = (f32[2,2,2,8,512]{4,3,2,1,0:T(8,128)S(1)}, f32[2,2,2,8,512]{4,3,2,1,0:T(8,128)S(1)}, u32[]{:S(2)}, u32[]{:S(2)}) collective-permute-start(f32[2,2,2,8,512]{4,3,2,1,0:T(8,128)S(1)} %get-tuple-element.36), channel_id=1, source_target_pairs={{32,0},{64,32},{96,64},{33,1},{65,33},{97,65},{34,2},{66,34},{98,6... | collective-permute-start | bytes 393224 | tf_op jit(solution)/shard_map/ppermute | solution.py:494
  81.3 0.0 copy-start.1
  81.3 9.4 %backward_own.1 = (f32[8,256,512]{2,1,0:T(8,128)}, f32[2,8,32,512]{3,2,1,0:T(8,128)S(1)}) custom-call(f32[8,256,512]{2,1,0:T(8,128)} %alpha_hbm.5, bf16[8,2,256,512]{3,2,1,0:T(8,128)(2,1)} %perts_hbm.5, f32[2,256,512]{2,1,0:T(8,128)S(1)} %bitcast.3, bf16[256,768]{1,0:T(8,128)(2,1)S(1)} %copy-done.3, bf16[2,1152,256]{2,1,0:T(8,128)(2,1)} %constant.8.clone.across_hbm.across_ref), custom_call_target="tpu_custom_call" | custom-call | flops 1000000 | tf_op jit(solution)/shard_map/backward_own/pallas_call | solution.py:367
  90.7 3.0 %collective-permute-done.5.pb_ref = f32[8,2,32,512]{3,2,1,0:T(8,128)} collective-permute-done((f32[8,2,32,512]{3,2,1,0:T(8,128)}, f32[8,2,32,512]{3,2,1,0:T(8,128)}, u32[]{:S(2)}, u32[]{:S(2)}) %collective-permute-start.5) | collective-permute-done | bytes 1048608 | tf_op jit(solution)/shard_map/ppermute | solution.py:494
  93.7 2.8 %collective-permute-done.7.ab_ref = f32[2,2,2,8,512]{4,3,2,1,0:T(8,128)S(1)} collective-permute-done((f32[2,2,2,8,512]{4,3,2,1,0:T(8,128)S(1)}, f32[2,2,2,8,512]{4,3,2,1,0:T(8,128)S(1)}, u32[]{:S(2)}, u32[]{:S(2)}) %collective-permute-start.7) | collective-permute-done | bytes 131104 | tf_op jit(solution)/shard_map/ppermute | solution.py:494
  96.5 3.5 %backward_edge.1 = f32[8,256,512]{2,1,0:T(8,128)} custom-call(f32[8,256,512]{2,1,0:T(8,128)} %get-tuple-element.31.grad_hbm, f32[2,8,32,512]{3,2,1,0:T(8,128)S(1)} %get-tuple-element.32.edge_ref, f32[8,2,32,512]{3,2,1,0:T(8,128)S(1)} %collective-permute-done.4.pt_ref, ...), custom_call_target="tpu_custom_call", output_to_operand_aliasing={{}: (0, {})} | custom-call | flops 1000000000 | bytes 6291456 | tf_op jit(solution)/shard_map/backward_edge/pallas_call | solution.py:403
  (18 shorter events, 0.0 us)
Async XLA Ops:
  0.0 21.6 %copy-start.3 = (bf16[256,768]{1,0:T(8,128)(2,1)S(1)}, bf16[256,768]{1,0:T(8,128)(2,1)}, u32[]{:S(2)}) copy-start(bf16[256,768]{1,0:T(8,128)(2,1)} %constant.6.clone.down_hbm) | copy-start | bytes 1179652
  3.6 26.5 %collective-permute-start = (f32[8,32,512]{2,1,0:T(8,128)}, f32[8,32,512]{2,1,0:T(8,128)}, u32[]{:S(2)}, u32[]{:S(2)}) collective-permute-start(f32[8,32,512]{2,1,0:T(8,128)} %get-tuple-element.21), channel_id=1, source_target_pairs={{0,32},{32,64},{64,96},{1,33},{33,65},{65,97},{2,34},{34,66},{66,9... | collective-permute-start | bytes 1572872 | tf_op jit(solution)/shard_map/ppermute | solution.py:494
  8.4 21.6 %collective-permute-start.1 = (f32[8,32,512]{2,1,0:T(8,128)}, f32[8,32,512]{2,1,0:T(8,128)}, u32[]{:S(2)}, u32[]{:S(2)}) collective-permute-start(f32[8,32,512]{2,1,0:T(8,128)} %get-tuple-element.22), channel_id=1, source_target_pairs={{32,0},{64,32},{96,64},{33,1},{65,33},{97,65},{34,2},{66,34},{98,6... | collective-permute-start | bytes 1572872 | tf_op jit(solution)/shard_map/ppermute | solution.py:494
  9.7 28.4 %all-to-all-start.1 = ((f32[128,2,768]{2,1,0:T(2,128)}), f32[128,2,768]{2,1,0:T(2,128)S(1)}, u32[]{:S(2)}, u32[]{:S(2)}) async-start(f32[128,2,768]{2,1,0:T(2,128)} %get-tuple-element.27), calls=%async_computation.1 | async-start | bytes 1572864 | tf_op jit(solution)/shard_map/all_to_all | solution.py:512
  21.6 8.5 %copy-start = (bf16[2,1152,256]{2,1,0:T(8,128)(2,1)S(1)}, bf16[2,1152,256]{2,1,0:T(8,128)(2,1)}, u32[]{:S(2)}) copy-start(bf16[2,1152,256]{2,1,0:T(8,128)(2,1)} %constant.8.clone.across_hbm.across_ref) | copy-start | bytes 3538948
  21.6 8.5 %copy-start.2 = (bf16[2,256,768]{2,1,0:T(8,128)(2,1)S(1)}, bf16[2,256,768]{2,1,0:T(8,128)(2,1)}, u32[]{:S(2)}) copy-start(bf16[2,256,768]{2,1,0:T(8,128)(2,1)} %constant.7.clone.down_ref) | copy-start | bytes 2359300
  21.6 8.5 %copy-start.4 = (bf16[8,2,32,512]{3,2,1,0:T(8,128)(2,1)S(1)}, bf16[8,2,32,512]{3,2,1,0:T(8,128)(2,1)}, u32[]{:S(2)}) copy-start(bf16[8,2,32,512]{3,2,1,0:T(8,128)(2,1)} %get-tuple-element.23.perts_first_ref.first_in_ref) | copy-start | bytes 1572868
  21.6 8.5 %copy-start.6 = (bf16[8,2,32,512]{3,2,1,0:T(8,128)(2,1)S(1)}, bf16[8,2,32,512]{3,2,1,0:T(8,128)(2,1)}, u32[]{:S(2)}) copy-start(bf16[8,2,32,512]{3,2,1,0:T(8,128)(2,1)} %get-tuple-element.24.perts_last_ref.last_in_ref) | copy-start | bytes 1572868
  32.7 2.7 %collective-permute-start.2 = (f32[16,2,8,512]{3,2,1,0:T(8,128)S(1)}, f32[16,2,8,512]{3,2,1,0:T(8,128)S(1)}, u32[]{:S(2)}, u32[]{:S(2)}) collective-permute-start(f32[16,2,8,512]{3,2,1,0:T(8,128)S(1)} %get-tuple-element.26), channel_id=1, source_target_pairs={{0,1},{1,0},{2,3},{3,2},{4,5},{5,4},{6,7},{7,6},{8,9},{9,8},{10,11... | collective-permute-start | bytes 1572872 | tf_op jit(solution)/shard_map/ppermute | solution.py:514
  38.1 18.7 %all-to-all-start = ((f32[16,2,8,512]{3,2,1,0:T(8,128)}), f32[16,2,8,512]{3,2,1,0:T(8,128)S(1)}, u32[]{:S(2)}, u32[]{:S(2)}) async-start(f32[16,2,8,512]{3,2,1,0:T(8,128)} %add.3), calls=%async_computation | async-start | bytes 1048576 | tf_op jit(solution)/shard_map/all_to_all | solution.py:498
  45.1 11.8 %copy-start.8 = (f32[2,8,512]{2,1,0:T(8,128)S(1)}, f32[2,8,512]{2,1,0:T(8,128)}, u32[]{:S(2)}) copy-start(f32[2,8,512]{2,1,0:T(8,128)} %back_ref.1) | copy-start | bytes 98308
  45.1 19.3 %copy-start.5 = (bf16[8,2,32,512]{3,2,1,0:T(8,128)(2,1)S(1)}, bf16[8,2,32,512]{3,2,1,0:T(8,128)(2,1)}, u32[]{:S(2)}) copy-start(bf16[8,2,32,512]{3,2,1,0:T(8,128)(2,1)} %get-tuple-element.23.perts_first_ref.first_in_ref) | copy-start | bytes 1572868
  57.7 17.0 %all-to-all-start.2 = ((f32[16,2,8,512]{3,2,1,0:T(8,128)}), f32[16,2,8,512]{3,2,1,0:T(8,128)S(1)}, u32[]{:S(2)}, u32[]{:S(2)}) async-start(f32[16,2,8,512]{3,2,1,0:T(8,128)} %adjoint.1.anchor_ref), calls=%async_computation.2 | async-start | bytes 1048576 | tf_op jit(solution)/shard_map/all_to_all | solution.py:498
  64.4 1.0 %copy-start.7 = (bf16[8,2,32,512]{3,2,1,0:T(8,128)(2,1)S(1)}, bf16[8,2,32,512]{3,2,1,0:T(8,128)(2,1)}, u32[]{:S(2)}) copy-start(bf16[8,2,32,512]{3,2,1,0:T(8,128)(2,1)} %get-tuple-element.24.perts_last_ref.last_in_ref) | copy-start | bytes 1572868
  66.9 23.8 %collective-permute-start.4 = (f32[8,2,32,512]{3,2,1,0:T(8,128)}, f32[8,2,32,512]{3,2,1,0:T(8,128)S(1)}, u32[]{:S(2)}, u32[]{:S(2)}) collective-permute-start(f32[8,2,32,512]{3,2,1,0:T(8,128)} %get-tuple-element.33), channel_id=1, source_target_pairs={{0,32},{32,64},{64,96},{1,33},{33,65},{65,97},{2,34},{34,66},{66,9... | collective-permute-start | bytes 3145736 | tf_op jit(solution)/shard_map/ppermute | solution.py:494
  68.2 25.5 %collective-permute-start.5 = (f32[8,2,32,512]{3,2,1,0:T(8,128)}, f32[8,2,32,512]{3,2,1,0:T(8,128)}, u32[]{:S(2)}, u32[]{:S(2)}) collective-permute-start(f32[8,2,32,512]{3,2,1,0:T(8,128)} %get-tuple-element.34), channel_id=1, source_target_pairs={{32,0},{64,32},{96,64},{33,1},{65,33},{97,65},{34,2},{66,34},{98,6... | collective-permute-start | bytes 3145736 | tf_op jit(solution)/shard_map/ppermute | solution.py:494
  74.7 3.7 %collective-permute-start.3 = (f32[16,2,8,512]{3,2,1,0:T(8,128)S(1)}, f32[16,2,8,512]{3,2,1,0:T(8,128)S(1)}, u32[]{:S(2)}, u32[]{:S(2)}) collective-permute-start(f32[16,2,8,512]{3,2,1,0:T(8,128)S(1)} %all-to-all-done.2.mine_ref), channel_id=1, source_target_pairs={{0,1},{1,0},{2,3},{3,2},{4,5},{5,4},{6,7},{7,6},{8,9},{9,8},{10,11... | collective-permute-start | bytes 1572872 | tf_op jit(solution)/shard_map/ppermute | solution.py:520
  78.5 15.2 %collective-permute-start.6 = (f32[2,2,2,8,512]{4,3,2,1,0:T(8,128)S(1)}, f32[2,2,2,8,512]{4,3,2,1,0:T(8,128)S(1)}, u32[]{:S(2)}, u32[]{:S(2)}) collective-permute-start(f32[2,2,2,8,512]{4,3,2,1,0:T(8,128)S(1)} %get-tuple-element.35), channel_id=1, source_target_pairs={{0,32},{32,64},{64,96},{1,33},{33,65},{65,97},{2,34},{34,66},{66,9... | collective-permute-start | bytes 393224 | tf_op jit(solution)/shard_map/ppermute | solution.py:494
  79.8 16.7 %collective-permute-start.7 = (f32[2,2,2,8,512]{4,3,2,1,0:T(8,128)S(1)}, f32[2,2,2,8,512]{4,3,2,1,0:T(8,128)S(1)}, u32[]{:S(2)}, u32[]{:S(2)}) collective-permute-start(f32[2,2,2,8,512]{4,3,2,1,0:T(8,128)S(1)} %get-tuple-element.36), channel_id=1, source_target_pairs={{32,0},{64,32},{96,64},{33,1},{65,33},{97,65},{34,2},{66,34},{98,6... | collective-permute-start | bytes 393224 | tf_op jit(solution)/shard_map/ppermute | solution.py:494
  81.3 15.3 %copy-start.1 = (bf16[2,1152,256]{2,1,0:T(8,128)(2,1)S(1)}, bf16[2,1152,256]{2,1,0:T(8,128)(2,1)}, u32[]{:S(2)}) copy-start(bf16[2,1152,256]{2,1,0:T(8,128)(2,1)} %constant.8.clone.across_hbm.across_ref) | copy-start | bytes 3538948

commit v3 on v2

--- a/solution.py
+++ b/solution.py
@@ -283,36 +283,23 @@
     )(back, got, w, v)
 
 
-def perts_edges_body(first_in_ref, last_in_ref, anchor_ref, first_ref, last_ref):
-    first_ref[...] = first_in_ref[...].astype(F32)
-    last_ref[...] = last_in_ref[...].astype(F32)
-
-
-def perts_edges(first, last, anchor):
-    return pl.pallas_call(
-        perts_edges_body, in_specs=[VMEM, VMEM, HBM], out_specs=[VMEM] * 2,
-        out_shape=[out(PERTS_EDGES), out(PERTS_EDGES)],
-        compiler_params=PARAMS, cost_estimate=cost(10**10, 0), name="perts_edges",
-    )(first, last, anchor)
-
-
-def assemble_body(mine_ref, other_ref, adj_ref, first_ref, last_ref):
+def assemble_body(mine_ref, other_ref, perts_first_ref, perts_last_ref, adj_ref, first_ref, last_ref):
     core = lax.rem(lax.axis_index("member"), 2)
     for field in range(2):
         adj_ref[field, :, core] = mine_ref[:, field]
         adj_ref[field, :, 1 - core] = other_ref[:, field]
-    for field in range(2):
-        first_ref[field] = adj_ref[field, :2]
-        last_ref[field] = adj_ref[field, 14:]
-
-
-def assemble(mine, other):
-    edge = out((2, 2, 2, SUB, COLS))
-    return pl.pallas_call(
-        assemble_body, in_specs=[VMEM] * 2, out_specs=[VMEM] * 3,
-        out_shape=[out((2, 16, 2, SUB, COLS)), edge, edge], compiler_params=PARAMS,
+    for at, p_ref, edge_ref in ((0, perts_first_ref, first_ref), (14, perts_last_ref, last_ref)):
+        rows = [adj_ref[field, at : at + 2].reshape(EDGE, COLS) for field in range(2)]
+        for m in range(MEMBERS):
+            edge_ref[m] = p_ref[m, 0].astype(F32) * rows[0] + p_ref[m, 1].astype(F32) * rows[1]
+
+
+def assemble(mine, other, perts_first, perts_last):
+    return pl.pallas_call(
+        assemble_body, in_specs=[VMEM] * 4, out_specs=[VMEM] * 3,
+        out_shape=[out(FIELD), out(EDGES), out(EDGES)], compiler_params=PARAMS,
         cost_estimate=cost(10**5, 2 * 2**20), name="assemble",
-    )(mine, other)
+    )(mine, other, perts_first, perts_last)
 
 
 def backward_body(
@@ -381,14 +368,9 @@
     )(alpha, perts, adj, down, across)
 
 
-def backward_edge_body(
-    grad_hbm, edge_ref, pt_ref, pb_ref, at_ref, ab_ref, down_ref, across_ref, out_hbm, scr, sems
-):
-    products = []
-    for p_ref, a_ref in ((pt_ref, at_ref), (pb_ref, ab_ref)):
-        first, second = [a_ref[field].reshape(1, EDGE, COLS) for field in range(2)]
-        products.append((p_ref[:, 0] * first + p_ref[:, 1] * second).reshape(MEMBERS * EDGE, COLS))
-    spread = conv(products, [down_ref[0], down_ref[1]], across_ref).reshape((2,) + EDGES)
+def backward_edge_body(grad_hbm, edge_ref, top_ref, bottom_ref, down_ref, across_ref, out_hbm, scr, sems):
+    halo = [ref[...].reshape(MEMBERS * EDGE, COLS) for ref in (top_ref, bottom_ref)]
+    spread = conv(halo, [down_ref[0], down_ref[1]], across_ref).reshape((2,) + EDGES)
     copies = []
     for side in range(2):
         scr[side] = edge_ref[side] + ENS_SCALE * spread[side]
@@ -399,10 +381,10 @@
         copy.wait()
 
 
-def backward_edge(grad, edge, pt, pb, at, ab, down, across):
+def backward_edge(grad, edge, top, bottom, down, across):
     return pl.pallas_call(
         backward_edge_body,
-        in_specs=[HBM] + [VMEM] * 7,
+        in_specs=[HBM] + [VMEM] * 5,
         out_specs=HBM,
         out_shape=out(grad.shape),
         input_output_aliases={0: 0},
@@ -410,21 +392,16 @@
         compiler_params=PARAMS,
         cost_estimate=cost(10**9, 6 * 2**20),
         name="backward_edge",
-    )(grad, edge, pt, pb, at, ab, down, across)
-
-
-SOURCES = 16
+    )(grad, edge, top, bottom, down, across)
+
+
+SOURCES = 128
 HIGH = 64
 LOW = 128
 
 
 def tables_body(got_ref, w_ref, v_ref, acc):
-    step = pl.program_id(0)
-
-    @pl.when(step == 0)
-    def _():
-        acc[...] = jnp.zeros_like(acc)
-
+    acc[...] = jnp.zeros_like(acc)
     index = lax.broadcasted_iota(jnp.int32, (16, 512), 0).astype(F32).astype(BF16)
     one = jnp.ones((16, 512), BF16)
     zero = jnp.zeros((16, 512), BF16)
@@ -457,25 +434,21 @@
         )
         return carry
 
-    lax.fori_loop(0, SOURCES, source, 0, unroll=8)
-
-    @pl.when(step == pl.num_programs(0) - 1)
-    def _():
-        for ref, base in ((w_ref, 0), (v_ref, 2 * HIGH)):
-            total = acc[base : base + HIGH] + acc[base + HIGH : base + 2 * HIGH]
-            for field in range(2):
-                for chunk in range(4):
-                    at = 16 * chunk + 8 * field
-                    ref[field, :, LOW * chunk : LOW * (chunk + 1)] = total[at : at + 8]
+    lax.fori_loop(0, SOURCES, source, 0, unroll=16)
+    for ref, base in ((w_ref, 0), (v_ref, 2 * HIGH)):
+        total = acc[base : base + HIGH] + acc[base + HIGH : base + 2 * HIGH]
+        for field in range(2):
+            for chunk in range(4):
+                at = 16 * chunk + 8 * field
+                ref[field, :, LOW * chunk : LOW * (chunk + 1)] = total[at : at + 8]
 
 
 def tables(got):
     piece = jax.ShapeDtypeStruct((2, SUB, COLS), F32)
     return pl.pallas_call(
         tables_body,
-        grid=(128 // SOURCES,),
-        in_specs=[pl.BlockSpec((SOURCES, 2, 768), lambda i: (i, 0, 0))],
-        out_specs=[whole((2, SUB, COLS))] * 2,
+        in_specs=[VMEM],
+        out_specs=[VMEM] * 2,
         out_shape=[piece, piece],
         scratch_shapes=[pltpu.VMEM((4 * HIGH, LOW), F32)],
         compiler_params=PARAMS,
@@ -515,12 +488,10 @@
     w_table, v_table = tables(got)
     adjoint = adjoint_of(background, pieces, w_table, v_table)
     mine = among_sixteen(adjoint)
-    first, last = perts_edges(perts_first, perts_last, adjoint)
-    perts_top, perts_bottom = exchange(last, first)
-    adj, first, last = assemble(mine, lax.ppermute(mine, "member", CORE))
-    adj_top, adj_bottom = exchange(last, first)
+    adj, first, last = assemble(mine, lax.ppermute(mine, "member", CORE), perts_first, perts_last)
+    top, bottom = exchange(last, first)
     grad, edge = backward(alpha, member_perts, adj.reshape(2, ROWS, COLS), down, across)
-    return backward_edge(grad, edge, perts_top, perts_bottom, adj_top, adj_bottom, edge_downs, across)
+    return backward_edge(grad, edge, top, bottom, edge_downs, across)
 
 
 def solution(mesh):

time: 102 us -> 96.1 us (0.942); the launches traced: 100 us -> 95.7 us
  blocking collectives: 0 us -> 16.9 us
  starting transfers between devices: 40.3 us -> 31.3 us
  waiting for transfers between devices: 16 us -> 8.53 us
  Pallas kernels: 41.6 us -> 37.7 us
  local copies, waits for them, and re-layouts: 1.08 us -> 0.04 us
    all_to_all x0 -> x1, blocking collectives: none -> 16.9 us  [among_sixteen(): lax.all_to_all(pieces, 'member', split_axis=0, concat_axis=0, axis_index_...]
    all_to_all x2 -> x1, starting transfers between devices: 13.6 us -> 6.86 us  [among_sixteen(): lax.all_to_all(pieces, 'member', split_axis=0, concat_axis=0, axis_index_...]
    all_to_all x2 -> x1, waiting for transfers between devices: 5.19 us -> 0.01 us  [among_sixteen(): lax.all_to_all(pieces, 'member', split_axis=0, concat_axis=0, axis_index_...]
    pallas_call x4 -> x3, Pallas kernels: 16.7 us -> 13.6 us  [the longest x1 11.2 us: tables(): pl.pallas_call(tables_body, in_specs=[VMEM], out_specs=[VMEM] * 2, out_sh...]
    ppermute x3 -> x2, waiting for transfers between devices: 5.85 us -> 3.83 us  [exchange(): lax.ppermute(first, 'region', DOWN)]
    ppermute x3 -> x2, starting transfers between devices: 7.49 us -> 6.16 us  [exchange(): lax.ppermute(last, 'region', UP)]
    ppermute x3 -> x2, starting transfers between devices: 4.04 us -> 2.75 us  [exchange(): lax.ppermute(first, 'region', DOWN)]
    unnamed x18 -> x14, local copies, waits for them, and re-layouts: 1.08 us -> 0.04 us
  transfers between devices with their start and end apart: 11 -> 8, of which waited for: 6 -> 5; matrix products, arithmetic and copies ran while one was open for 1% -> 1% of each run, Pallas kernels for 34% -> 33%
where the time goes in v3:
time: 96.1 us; the launch traced here: 95.7 us
  Pallas kernels  37.7 us (39%)
  starting transfers between devices  31.3 us (33%)
  blocking collectives  16.9 us (18%)
  waiting for transfers between devices  8.53 us (9%)
    all_to_all x1, blocking collectives, among_sixteen(): lax.all_to_all(pieces, 'member', split_axis=0, concat_axis=0, axis_index_...  16.9 us
    all_to_all x1, starting transfers between devices, body(): lax.all_to_all(send, ('region', 'member'), split_axis=0, concat_axis=0, t...  12.3 us
    pallas_call x1, Pallas kernels, tables(): pl.pallas_call(tables_body, in_specs=[VMEM], out_specs=[VMEM] * 2, out_sh...  11.2 us
    pallas_call x1, Pallas kernels, backward(): pl.pallas_call(backward_body, in_specs=[HBM, HBM, VMEM, HBM, HBM], out_sp...  9.4 us
    pallas_call x1, Pallas kernels, forward(): pl.pallas_call(forward_body, in_specs=[HBM] * 4, out_specs=VMEM, out_shap...  8.42 us
    all_to_all x1, starting transfers between devices, among_sixteen(): lax.all_to_all(pieces, 'member', split_axis=0, concat_axis=0, axis_index_...  6.86 us
    ppermute x2, starting transfers between devices, exchange(): lax.ppermute(last, 'region', UP)  6.16 us
    ppermute x2, waiting for transfers between devices, exchange(): lax.ppermute(first, 'region', DOWN)  3.83 us
  transfers between devices with their start and end apart: 8, of which 5 were waited for; matrix products, arithmetic and copies ran while one was open for 1% of the time, Pallas kernels for 33%

profile of v3, /device:TPU:1, one launch (start us, length us, event | category | flops | bytes accessed | tf_op | source)
XLA Modules:
  0.0 95.7 jit_solution(13030194332740372637)
XLA Ops:
  0.0 3.6 %place.1 = (f32[128,2,768]{2,1,0:T(2,128)}, f32[8,32,512]{2,1,0:T(8,128)}, f32[8,32,512]{2,1,0:T(8,128)}, bf16[8,2,32,512]{3,2,1,0:T(8,128)(2,1)}, bf16[8,2,32,512]{3,2,1,0:T(8,128)(2,1)}) custom-call(s32[112]{0:T(128)} %bitcast.4, s32[112]{0:T(128)} %bitcast.5, f32[1,112,256]{2,1,0:T(8,128)} %value_hbm.1, f32[1,112,256]{2,1,0:T(8,128)} %weight_hbm.1, ...), custom_call_target="tpu_custom_call" | custom-call | flops 1000000000 | tf_op jit(solution)/shard_map/place/pallas_call | solution.py:155
  3.6 4.8 %collective-permute-start = (f32[8,32,512]{2,1,0:T(8,128)}, f32[8,32,512]{2,1,0:T(8,128)}, u32[]{:S(2)}, u32[]{:S(2)}) collective-permute-start(f32[8,32,512]{2,1,0:T(8,128)} %get-tuple-element.19), channel_id=1, source_target_pairs={{0,32},{32,64},{64,96},{1,33},{33,65},{65,97},{2,34},{34,66},{66,9... | collective-permute-start | bytes 1572872 | tf_op jit(solution)/shard_map/ppermute | solution.py:467
  8.4 1.3 %collective-permute-start.1 = (f32[8,32,512]{2,1,0:T(8,128)}, f32[8,32,512]{2,1,0:T(8,128)}, u32[]{:S(2)}, u32[]{:S(2)}) collective-permute-start(f32[8,32,512]{2,1,0:T(8,128)} %get-tuple-element.20), channel_id=1, source_target_pairs={{32,0},{64,32},{96,64},{33,1},{65,33},{97,65},{34,2},{66,34},{98,6... | collective-permute-start | bytes 1572872 | tf_op jit(solution)/shard_map/ppermute | solution.py:467
  9.7 12.3 %all-to-all-start.1 = ((f32[128,2,768]{2,1,0:T(2,128)}), f32[128,2,768]{2,1,0:T(2,128)}, u32[]{:S(2)}, u32[]{:S(2)}) async-start(f32[128,2,768]{2,1,0:T(2,128)} %get-tuple-element.25), calls=%async_computation.1 | async-start | bytes 1572864 | tf_op jit(solution)/shard_map/all_to_all | solution.py:485
  22.0 0.0 copy-done.5
  22.0 0.0 copy-start
  22.0 0.0 copy-start.2
  22.0 0.0 copy-start.3
  22.0 8.4 %forward.1.term_ref = f32[2,16,2,8,512]{4,3,2,1,0:T(8,128)S(1)} custom-call(f32[8,256,512]{2,1,0:T(8,128)} %alpha_hbm.5, bf16[8,2,256,512]{3,2,1,0:T(8,128)(2,1)} %perts_hbm.5, bf16[256,768]{1,0:T(8,128)(2,1)S(1)} %copy-done.5, bf16[2,1152,256]{2,1,0:T(8,128)(2,1)} %constant.8.clone.across_hbm.across_ref), custom_call_target="tpu_custom_call" | custom-call | flops 1000000 | tf_op jit(solution)/shard_map/forward/pallas_call | solution.py:227
  30.4 0.0 collective-permute-done.top_ref
  30.5 0.0 collective-permute-done.1.bottom_ref
  30.5 2.6 %forward_edge.1 = (f32[16,2,8,512]{3,2,1,0:T(8,128)S(1)}, f32[16,2,8,512]{3,2,1,0:T(8,128)S(1)}) custom-call(f32[2,16,2,8,512]{4,3,2,1,0:T(8,128)S(1)} %forward.1.term_ref, f32[8,32,512]{2,1,0:T(8,128)} %collective-permute-done.top_ref, f32[8,32,512]{2,1,0:T(8,128)} %collective-permute-done.1.bottom_ref, bf16[8,2,32,512]{3,2,1,0:T(8,128)(2,1)S(1)} %copy-done.3, ...), custom_call_target="tpu_custom_call" | custom-call | flops 1000000000 | bytes 6291456 | tf_op jit(solution)/shard_map/forward_edge/pallas_call | solution.py:263
  33.1 1.2 %collective-permute-start.2 = (f32[16,2,8,512]{3,2,1,0:T(8,128)S(1)}, f32[16,2,8,512]{3,2,1,0:T(8,128)S(1)}, u32[]{:S(2)}, u32[]{:S(2)}) collective-permute-start(f32[16,2,8,512]{3,2,1,0:T(8,128)S(1)} %get-tuple-element.24), channel_id=1, source_target_pairs={{0,1},{1,0},{2,3},{3,2},{4,5},{5,4},{6,7},{7,6},{8,9},{9,8},{10,11... | collective-permute-start | bytes 1572872 | tf_op jit(solution)/shard_map/ppermute | solution.py:487
  34.3 1.5 %collective-permute-done.2 = f32[16,2,8,512]{3,2,1,0:T(8,128)S(1)} collective-permute-done((f32[16,2,8,512]{3,2,1,0:T(8,128)S(1)}, f32[16,2,8,512]{3,2,1,0:T(8,128)S(1)}, u32[]{:S(2)}, u32[]{:S(2)}) %collective-permute-start.2) | collective-permute-done | bytes 524320 | tf_op jit(solution)/shard_map/ppermute | solution.py:487
  35.8 0.9 add.3
  36.7 1.5 %all-to-all-done.1.got_ref = f32[128,2,768]{2,1,0:T(2,128)} async-done(((f32[128,2,768]{2,1,0:T(2,128)}), f32[128,2,768]{2,1,0:T(2,128)}, u32[]{:S(2)}, u32[]{:S(2)}) %all-to-all-start.1) | async-done | bytes 786464 | tf_op jit(solution)/shard_map/all_to_all | solution.py:485
  38.2 6.9 %all-to-all-start = ((f32[16,2,8,512]{3,2,1,0:T(8,128)}), f32[16,2,8,512]{3,2,1,0:T(8,128)S(1)}, u32[]{:S(2)}, u32[]{:S(2)}) async-start(f32[16,2,8,512]{3,2,1,0:T(8,128)} %add.3), calls=%async_computation | async-start | bytes 1048576 | tf_op jit(solution)/shard_map/all_to_all | solution.py:471
  45.1 0.0 copy-start.6
  45.1 11.2 %weight_tables.1 = (f32[2,8,512]{2,1,0:T(8,128)S(1)}, f32[2,8,512]{2,1,0:T(8,128)S(1)}) custom-call(f32[128,2,768]{2,1,0:T(2,128)} %all-to-all-done.1.got_ref), custom_call_target="tpu_custom_call" | custom-call | flops 12000000000 | bytes 1048576 | tf_op jit(solution)/shard_map/weight_tables/pallas_call | solution.py:448
  56.3 0.0 all-to-all-done.got_ref
  56.3 0.1 adjoint.1
  56.4 16.9 %all_to_all.15.mine_ref = f32[16,2,8,512]{3,2,1,0:T(8,128)S(1)} all-to-all(f32[16,2,8,512]{3,2,1,0:T(8,128)S(1)} %adjoint.1), channel_id=1, replica_groups={{0,2,4,6,8,10,12,14,16,18,20,22,24,26,28,30},{1,3,5,7,9,11,13,15,17,19,..., dimensions={0} | all-to-all | bytes 1048576 | tf_op jit(solution)/shard_map/all_to_all | solution.py:471
  73.2 2.1 %collective-permute-start.3 = (f32[16,2,8,512]{3,2,1,0:T(8,128)S(1)}, f32[16,2,8,512]{3,2,1,0:T(8,128)S(1)}, u32[]{:S(2)}, u32[]{:S(2)}) collective-permute-start(f32[16,2,8,512]{3,2,1,0:T(8,128)S(1)} %all_to_all.15.mine_ref), channel_id=1, source_target_pairs={{0,1},{1,0},{2,3},{3,2},{4,5},{5,4},{6,7},{7,6},{8,9},{9,8},{10,11... | collective-permute-start | bytes 1572872 | tf_op jit(solution)/shard_map/ppermute | solution.py:491
  75.3 1.5 %collective-permute-done.3.other_ref = f32[16,2,8,512]{3,2,1,0:T(8,128)S(1)} collective-permute-done((f32[16,2,8,512]{3,2,1,0:T(8,128)S(1)}, f32[16,2,8,512]{3,2,1,0:T(8,128)S(1)}, u32[]{:S(2)}, u32[]{:S(2)}) %collective-permute-start.3) | collective-permute-done | bytes 524320 | tf_op jit(solution)/shard_map/ppermute | solution.py:491
  76.9 0.3 assemble.1
  77.1 1.3 %collective-permute-start.4 = (f32[8,32,512]{2,1,0:T(8,128)S(1)}, f32[8,32,512]{2,1,0:T(8,128)S(1)}, u32[]{:S(2)}, u32[]{:S(2)}) collective-permute-start(f32[8,32,512]{2,1,0:T(8,128)S(1)} %get-tuple-element.31), channel_id=1, source_target_pairs={{0,32},{32,64},{64,96},{1,33},{33,65},{65,97},{2,34},{34,66},{66,9... | collective-permute-start | bytes 1572872 | tf_op jit(solution)/shard_map/ppermute | solution.py:467
  78.4 1.5 %collective-permute-start.5 = (f32[8,32,512]{2,1,0:T(8,128)S(1)}, f32[8,32,512]{2,1,0:T(8,128)S(1)}, u32[]{:S(2)}, u32[]{:S(2)}) collective-permute-start(f32[8,32,512]{2,1,0:T(8,128)S(1)} %get-tuple-element.32), channel_id=1, source_target_pairs={{32,0},{64,32},{96,64},{33,1},{65,33},{97,65},{34,2},{66,34},{98,6... | collective-permute-start | bytes 1572872 | tf_op jit(solution)/shard_map/ppermute | solution.py:467
  79.9 0.0 copy-start.1
  79.9 9.4 %backward_own.1 = (f32[8,256,512]{2,1,0:T(8,128)}, f32[2,8,32,512]{3,2,1,0:T(8,128)S(1)}) custom-call(f32[8,256,512]{2,1,0:T(8,128)} %alpha_hbm.5, bf16[8,2,256,512]{3,2,1,0:T(8,128)(2,1)} %perts_hbm.5, f32[2,256,512]{2,1,0:T(8,128)S(1)} %bitcast.3, bf16[256,768]{1,0:T(8,128)(2,1)S(1)} %copy-done.5, bf16[2,1152,256]{2,1,0:T(8,128)(2,1)} %constant.8.clone.across_hbm.across_ref), custom_call_target="tpu_custom_call" | custom-call | flops 1000000 | tf_op jit(solution)/shard_map/backward_own/pallas_call | solution.py:354
  89.3 0.1 collective-permute-done.4.top_ref
  89.5 3.8 %collective-permute-done.5.bottom_ref = f32[8,32,512]{2,1,0:T(8,128)S(1)} collective-permute-done((f32[8,32,512]{2,1,0:T(8,128)S(1)}, f32[8,32,512]{2,1,0:T(8,128)S(1)}, u32[]{:S(2)}, u32[]{:S(2)}) %collective-permute-start.5) | collective-permute-done | bytes 524320 | tf_op jit(solution)/shard_map/ppermute | solution.py:467
  93.3 2.2 %backward_edge.1 = f32[8,256,512]{2,1,0:T(8,128)} custom-call(f32[8,256,512]{2,1,0:T(8,128)} %get-tuple-element.29.grad_hbm, f32[2,8,32,512]{3,2,1,0:T(8,128)S(1)} %get-tuple-element.30.edge_ref, f32[8,32,512]{2,1,0:T(8,128)S(1)} %collective-permute-done.4.top_ref, ...), custom_call_target="tpu_custom_call", output_to_operand_aliasing={{}: (0, {})} | custom-call | flops 1000000000 | bytes 6291456 | tf_op jit(solution)/shard_map/backward_edge/pallas_call | solution.py:385
  (8 shorter events, 0.0 us)
Async XLA Ops:
  0.0 22.0 %copy-start.5 = (bf16[256,768]{1,0:T(8,128)(2,1)S(1)}, bf16[256,768]{1,0:T(8,128)(2,1)}, u32[]{:S(2)}) copy-start(bf16[256,768]{1,0:T(8,128)(2,1)} %constant.6.clone.down_hbm) | copy-start | bytes 1179652
  3.6 26.9 %collective-permute-start = (f32[8,32,512]{2,1,0:T(8,128)}, f32[8,32,512]{2,1,0:T(8,128)}, u32[]{:S(2)}, u32[]{:S(2)}) collective-permute-start(f32[8,32,512]{2,1,0:T(8,128)} %get-tuple-element.19), channel_id=1, source_target_pairs={{0,32},{32,64},{64,96},{1,33},{33,65},{65,97},{2,34},{34,66},{66,9... | collective-permute-start | bytes 1572872 | tf_op jit(solution)/shard_map/ppermute | solution.py:467
  8.4 22.0 %collective-permute-start.1 = (f32[8,32,512]{2,1,0:T(8,128)}, f32[8,32,512]{2,1,0:T(8,128)}, u32[]{:S(2)}, u32[]{:S(2)}) collective-permute-start(f32[8,32,512]{2,1,0:T(8,128)} %get-tuple-element.20), channel_id=1, source_target_pairs={{32,0},{64,32},{96,64},{33,1},{65,33},{97,65},{34,2},{66,34},{98,6... | collective-permute-start | bytes 1572872 | tf_op jit(solution)/shard_map/ppermute | solution.py:467
  9.7 28.5 %all-to-all-start.1 = ((f32[128,2,768]{2,1,0:T(2,128)}), f32[128,2,768]{2,1,0:T(2,128)}, u32[]{:S(2)}, u32[]{:S(2)}) async-start(f32[128,2,768]{2,1,0:T(2,128)} %get-tuple-element.25), calls=%async_computation.1 | async-start | bytes 1572864 | tf_op jit(solution)/shard_map/all_to_all | solution.py:485
  22.0 8.5 %copy-start = (bf16[2,1152,256]{2,1,0:T(8,128)(2,1)S(1)}, bf16[2,1152,256]{2,1,0:T(8,128)(2,1)}, u32[]{:S(2)}) copy-start(bf16[2,1152,256]{2,1,0:T(8,128)(2,1)} %constant.8.clone.across_hbm.across_ref) | copy-start | bytes 3538948
  22.0 8.5 %copy-start.2 = (bf16[2,256,768]{2,1,0:T(8,128)(2,1)S(1)}, bf16[2,256,768]{2,1,0:T(8,128)(2,1)}, u32[]{:S(2)}) copy-start(bf16[2,256,768]{2,1,0:T(8,128)(2,1)} %constant.7.clone.down_ref) | copy-start | bytes 2359300
  22.0 8.5 %copy-start.3 = (bf16[8,2,32,512]{3,2,1,0:T(8,128)(2,1)S(1)}, bf16[8,2,32,512]{3,2,1,0:T(8,128)(2,1)}, u32[]{:S(2)}) copy-start(bf16[8,2,32,512]{3,2,1,0:T(8,128)(2,1)} %get-tuple-element.21.perts_first_ref) | copy-start | bytes 1572868
  22.0 8.5 %copy-start.4 = (bf16[8,2,32,512]{3,2,1,0:T(8,128)(2,1)S(1)}, bf16[8,2,32,512]{3,2,1,0:T(8,128)(2,1)}, u32[]{:S(2)}) copy-start(bf16[8,2,32,512]{3,2,1,0:T(8,128)(2,1)} %get-tuple-element.22.perts_last_ref) | copy-start | bytes 1572868
  33.1 2.7 %collective-permute-start.2 = (f32[16,2,8,512]{3,2,1,0:T(8,128)S(1)}, f32[16,2,8,512]{3,2,1,0:T(8,128)S(1)}, u32[]{:S(2)}, u32[]{:S(2)}) collective-permute-start(f32[16,2,8,512]{3,2,1,0:T(8,128)S(1)} %get-tuple-element.24), channel_id=1, source_target_pairs={{0,1},{1,0},{2,3},{3,2},{4,5},{5,4},{6,7},{7,6},{8,9},{9,8},{10,11... | collective-permute-start | bytes 1572872 | tf_op jit(solution)/shard_map/ppermute | solution.py:487
  38.2 18.1 %all-to-all-start = ((f32[16,2,8,512]{3,2,1,0:T(8,128)}), f32[16,2,8,512]{3,2,1,0:T(8,128)S(1)}, u32[]{:S(2)}, u32[]{:S(2)}) async-start(f32[16,2,8,512]{3,2,1,0:T(8,128)} %add.3), calls=%async_computation | async-start | bytes 1048576 | tf_op jit(solution)/shard_map/all_to_all | solution.py:471
  45.1 11.2 %copy-start.6 = (f32[2,8,512]{2,1,0:T(8,128)S(1)}, f32[2,8,512]{2,1,0:T(8,128)}, u32[]{:S(2)}) copy-start(f32[2,8,512]{2,1,0:T(8,128)} %back_ref.1) | copy-start | bytes 98308
  73.2 3.6 %collective-permute-start.3 = (f32[16,2,8,512]{3,2,1,0:T(8,128)S(1)}, f32[16,2,8,512]{3,2,1,0:T(8,128)S(1)}, u32[]{:S(2)}, u32[]{:S(2)}) collective-permute-start(f32[16,2,8,512]{3,2,1,0:T(8,128)S(1)} %all_to_all.15.mine_ref), channel_id=1, source_target_pairs={{0,1},{1,0},{2,3},{3,2},{4,5},{5,4},{6,7},{7,6},{8,9},{9,8},{10,11... | collective-permute-start | bytes 1572872 | tf_op jit(solution)/shard_map/ppermute | solution.py:491
  77.1 12.4 %collective-permute-start.4 = (f32[8,32,512]{2,1,0:T(8,128)S(1)}, f32[8,32,512]{2,1,0:T(8,128)S(1)}, u32[]{:S(2)}, u32[]{:S(2)}) collective-permute-start(f32[8,32,512]{2,1,0:T(8,128)S(1)} %get-tuple-element.31), channel_id=1, source_target_pairs={{0,32},{32,64},{64,96},{1,33},{33,65},{65,97},{2,34},{34,66},{66,9... | collective-permute-start | bytes 1572872 | tf_op jit(solution)/shard_map/ppermute | solution.py:467
  78.4 14.9 %collective-permute-start.5 = (f32[8,32,512]{2,1,0:T(8,128)S(1)}, f32[8,32,512]{2,1,0:T(8,128)S(1)}, u32[]{:S(2)}, u32[]{:S(2)}) collective-permute-start(f32[8,32,512]{2,1,0:T(8,128)S(1)} %get-tuple-element.32), channel_id=1, source_target_pairs={{32,0},{64,32},{96,64},{33,1},{65,33},{97,65},{34,2},{66,34},{98,6... | collective-permute-start | bytes 1572872 | tf_op jit(solution)/shard_map/ppermute | solution.py:467
  79.9 13.4 %copy-start.1 = (bf16[2,1152,256]{2,1,0:T(8,128)(2,1)S(1)}, bf16[2,1152,256]{2,1,0:T(8,128)(2,1)}, u32[]{:S(2)}) copy-start(bf16[2,1152,256]{2,1,0:T(8,128)(2,1)} %constant.8.clone.across_hbm.across_ref) | copy-start | bytes 3538948

commit v4 on v3

--- a/solution.py
+++ b/solution.py
@@ -1,3 +1,4 @@
+import functools
 import math
 
 import jax
@@ -368,31 +369,28 @@
     )(alpha, perts, adj, down, across)
 
 
-def backward_edge_body(grad_hbm, edge_ref, top_ref, bottom_ref, down_ref, across_ref, out_hbm, scr, sems):
-    halo = [ref[...].reshape(MEMBERS * EDGE, COLS) for ref in (top_ref, bottom_ref)]
-    spread = conv(halo, [down_ref[0], down_ref[1]], across_ref).reshape((2,) + EDGES)
-    copies = []
-    for side in range(2):
-        scr[side] = edge_ref[side] + ENS_SCALE * spread[side]
-        at = (ROWS - EDGE) * side
-        copies.append(pltpu.make_async_copy(scr.at[side], out_hbm.at[:, at : at + EDGE, :], sems.at[side]))
-        copies[side].start()
-    for copy in copies:
-        copy.wait()
-
-
-def backward_edge(grad, edge, top, bottom, down, across):
-    return pl.pallas_call(
-        backward_edge_body,
-        in_specs=[HBM] + [VMEM] * 5,
+def backward_edge_body(side, grad_hbm, edge_ref, halo_ref, down_ref, across_ref, out_hbm, scr, sem):
+    halo = halo_ref[...].reshape(MEMBERS * EDGE, COLS)
+    spread = conv([halo], [down_ref[side]], across_ref).reshape(EDGES)
+    scr[...] = edge_ref[side] + ENS_SCALE * spread
+    at = (ROWS - EDGE) * side
+    copy = pltpu.make_async_copy(scr, out_hbm.at[:, at : at + EDGE, :], sem)
+    copy.start()
+    copy.wait()
+
+
+def backward_edge(side, grad, edge, halo, down, across):
+    return pl.pallas_call(
+        functools.partial(backward_edge_body, side),
+        in_specs=[HBM] + [VMEM] * 4,
         out_specs=HBM,
         out_shape=out(grad.shape),
         input_output_aliases={0: 0},
-        scratch_shapes=[pltpu.VMEM((2,) + EDGES, F32), pltpu.SemaphoreType.DMA((2,))],
+        scratch_shapes=[pltpu.VMEM(EDGES, F32), pltpu.SemaphoreType.DMA(())],
         compiler_params=PARAMS,
-        cost_estimate=cost(10**9, 6 * 2**20),
+        cost_estimate=cost(5 * 10**8, 3 * 2**20),
         name="backward_edge",
-    )(grad, edge, top, bottom, down, across)
+    )(grad, edge, halo, down, across)
 
 
 SOURCES = 128
@@ -491,7 +489,8 @@
     adj, first, last = assemble(mine, lax.ppermute(mine, "member", CORE), perts_first, perts_last)
     top, bottom = exchange(last, first)
     grad, edge = backward(alpha, member_perts, adj.reshape(2, ROWS, COLS), down, across)
-    return backward_edge(grad, edge, top, bottom, edge_downs, across)
+    grad = backward_edge(0, grad, edge, top, edge_downs, across)
+    return backward_edge(1, grad, edge, bottom, edge_downs, across)
 
 
 def solution(mesh):

time: 96.1 us -> 95.5 us (level)
  waiting for transfers between devices: 8.53 us -> 6.92 us
  Pallas kernels: 37.7 us -> 38.7 us
    ppermute x2, waiting for transfers between devices: 3.83 us -> 2.22 us  [exchange(): lax.ppermute(first, 'region', DOWN)]
    pallas_call x1 -> x2, Pallas kernels: 2.18 us -> 3.2 us  [backward_edge(): pl.pallas_call(functools.partial(backward_edge_body, side), in_specs=[HBM...]
  transfers between devices with their start and end apart: 8 -> 8, of which waited for: 5 -> 5; matrix products, arithmetic and copies ran while one was open for 1% -> 1% of each run, Pallas kernels for 33% -> 35%
where the time goes in v4:
time: 95.5 us; the launch traced here: 95.1 us
  Pallas kernels  38.7 us (41%)
  starting transfers between devices  31.3 us (33%)
  blocking collectives  16.9 us (18%)
  waiting for transfers between devices  6.92 us (7%)
    all_to_all x1, blocking collectives, among_sixteen(): lax.all_to_all(pieces, 'member', split_axis=0, concat_axis=0, axis_index_...  16.9 us
    all_to_all x1, starting transfers between devices, body(): lax.all_to_all(send, ('region', 'member'), split_axis=0, concat_axis=0, t...  12.3 us
    pallas_call x1, Pallas kernels, tables(): pl.pallas_call(tables_body, in_specs=[VMEM], out_specs=[VMEM] * 2, out_sh...  11.2 us
    pallas_call x1, Pallas kernels, backward(): pl.pallas_call(backward_body, in_specs=[HBM, HBM, VMEM, HBM, HBM], out_sp...  9.4 us
    pallas_call x1, Pallas kernels, forward(): pl.pallas_call(forward_body, in_specs=[HBM] * 4, out_specs=VMEM, out_shap...  8.42 us
    all_to_all x1, starting transfers between devices, among_sixteen(): lax.all_to_all(pieces, 'member', split_axis=0, concat_axis=0, axis_index_...  6.86 us
    ppermute x2, starting transfers between devices, exchange(): lax.ppermute(last, 'region', UP)  6.16 us
    pallas_call x1, Pallas kernels, place(): pl.pallas_call(place_body, in_specs=[HBM] * 7, out_specs=[VMEM] * 5, out_...  3.57 us
  transfers between devices with their start and end apart: 8, of which 5 were waited for; matrix products, arithmetic and copies ran while one was open for 1% of the time, Pallas kernels for 35%

profile of v4, /device:TPU:1, one launch (start us, length us, event | category | flops | bytes accessed | tf_op | source)
XLA Modules:
  0.0 95.1 jit_solution(1285516981881192909)
XLA Ops:
  0.0 3.6 %place.1 = (f32[128,2,768]{2,1,0:T(2,128)}, f32[8,32,512]{2,1,0:T(8,128)}, f32[8,32,512]{2,1,0:T(8,128)}, bf16[8,2,32,512]{3,2,1,0:T(8,128)(2,1)}, bf16[8,2,32,512]{3,2,1,0:T(8,128)(2,1)}) custom-call(s32[112]{0:T(128)} %bitcast.4, s32[112]{0:T(128)} %bitcast.5, f32[1,112,256]{2,1,0:T(8,128)} %value_hbm.1, f32[1,112,256]{2,1,0:T(8,128)} %weight_hbm.1, ...), custom_call_target="tpu_custom_call" | custom-call | flops 1000000000 | tf_op jit(solution)/shard_map/place/pallas_call | solution.py:156
  3.6 4.8 %collective-permute-start = (f32[8,32,512]{2,1,0:T(8,128)}, f32[8,32,512]{2,1,0:T(8,128)}, u32[]{:S(2)}, u32[]{:S(2)}) collective-permute-start(f32[8,32,512]{2,1,0:T(8,128)} %get-tuple-element.19), channel_id=1, source_target_pairs={{0,32},{32,64},{64,96},{1,33},{33,65},{65,97},{2,34},{34,66},{66,9... | collective-permute-start | bytes 1572872 | tf_op jit(solution)/shard_map/ppermute | solution.py:465
  8.4 1.3 %collective-permute-start.1 = (f32[8,32,512]{2,1,0:T(8,128)}, f32[8,32,512]{2,1,0:T(8,128)}, u32[]{:S(2)}, u32[]{:S(2)}) collective-permute-start(f32[8,32,512]{2,1,0:T(8,128)} %get-tuple-element.20), channel_id=1, source_target_pairs={{32,0},{64,32},{96,64},{33,1},{65,33},{97,65},{34,2},{66,34},{98,6... | collective-permute-start | bytes 1572872 | tf_op jit(solution)/shard_map/ppermute | solution.py:465
  9.7 12.3 %all-to-all-start.1 = ((f32[128,2,768]{2,1,0:T(2,128)}), f32[128,2,768]{2,1,0:T(2,128)}, u32[]{:S(2)}, u32[]{:S(2)}) async-start(f32[128,2,768]{2,1,0:T(2,128)} %get-tuple-element.25), calls=%async_computation.1 | async-start | bytes 1572864 | tf_op jit(solution)/shard_map/all_to_all | solution.py:483
  22.0 0.0 copy-done.5
  22.0 0.0 copy-start
  22.0 0.0 copy-start.2
  22.0 8.4 %forward.1.term_ref = f32[2,16,2,8,512]{4,3,2,1,0:T(8,128)S(1)} custom-call(f32[8,256,512]{2,1,0:T(8,128)} %alpha_hbm.5, bf16[8,2,256,512]{3,2,1,0:T(8,128)(2,1)} %perts_hbm.5, bf16[256,768]{1,0:T(8,128)(2,1)S(1)} %copy-done.5, bf16[2,1152,256]{2,1,0:T(8,128)(2,1)} %constant.8.clone.across_hbm.across_ref), custom_call_target="tpu_custom_call" | custom-call | flops 1000000 | tf_op jit(solution)/shard_map/forward/pallas_call | solution.py:228
  30.4 0.0 collective-permute-done.top_ref
  30.5 0.0 collective-permute-done.1.bottom_ref
  30.5 2.6 %forward_edge.1 = (f32[16,2,8,512]{3,2,1,0:T(8,128)S(1)}, f32[16,2,8,512]{3,2,1,0:T(8,128)S(1)}) custom-call(f32[2,16,2,8,512]{4,3,2,1,0:T(8,128)S(1)} %forward.1.term_ref, f32[8,32,512]{2,1,0:T(8,128)} %collective-permute-done.top_ref, f32[8,32,512]{2,1,0:T(8,128)} %collective-permute-done.1.bottom_ref, bf16[8,2,32,512]{3,2,1,0:T(8,128)(2,1)S(1)} %copy-done.3, ...), custom_call_target="tpu_custom_call" | custom-call | flops 1000000000 | bytes 6291456 | tf_op jit(solution)/shard_map/forward_edge/pallas_call | solution.py:264
  33.1 1.2 %collective-permute-start.2 = (f32[16,2,8,512]{3,2,1,0:T(8,128)S(1)}, f32[16,2,8,512]{3,2,1,0:T(8,128)S(1)}, u32[]{:S(2)}, u32[]{:S(2)}) collective-permute-start(f32[16,2,8,512]{3,2,1,0:T(8,128)S(1)} %get-tuple-element.24), channel_id=1, source_target_pairs={{0,1},{1,0},{2,3},{3,2},{4,5},{5,4},{6,7},{7,6},{8,9},{9,8},{10,11... | collective-permute-start | bytes 1572872 | tf_op jit(solution)/shard_map/ppermute | solution.py:485
  34.3 1.5 %collective-permute-done.2 = f32[16,2,8,512]{3,2,1,0:T(8,128)S(1)} collective-permute-done((f32[16,2,8,512]{3,2,1,0:T(8,128)S(1)}, f32[16,2,8,512]{3,2,1,0:T(8,128)S(1)}, u32[]{:S(2)}, u32[]{:S(2)}) %collective-permute-start.2) | collective-permute-done | bytes 524320 | tf_op jit(solution)/shard_map/ppermute | solution.py:485
  35.8 0.9 add.3
  36.7 1.5 %all-to-all-done.1.got_ref = f32[128,2,768]{2,1,0:T(2,128)} async-done(((f32[128,2,768]{2,1,0:T(2,128)}), f32[128,2,768]{2,1,0:T(2,128)}, u32[]{:S(2)}, u32[]{:S(2)}) %all-to-all-start.1) | async-done | bytes 786464 | tf_op jit(solution)/shard_map/all_to_all | solution.py:483
  38.2 6.9 %all-to-all-start = ((f32[16,2,8,512]{3,2,1,0:T(8,128)}), f32[16,2,8,512]{3,2,1,0:T(8,128)S(1)}, u32[]{:S(2)}, u32[]{:S(2)}) async-start(f32[16,2,8,512]{3,2,1,0:T(8,128)} %add.3), calls=%async_computation | async-start | bytes 1048576 | tf_op jit(solution)/shard_map/all_to_all | solution.py:469
  45.1 0.0 copy-start.6
  45.1 11.2 %weight_tables.1 = (f32[2,8,512]{2,1,0:T(8,128)S(1)}, f32[2,8,512]{2,1,0:T(8,128)S(1)}) custom-call(f32[128,2,768]{2,1,0:T(2,128)} %all-to-all-done.1.got_ref), custom_call_target="tpu_custom_call" | custom-call | flops 12000000000 | bytes 1048576 | tf_op jit(solution)/shard_map/weight_tables/pallas_call | solution.py:446
  56.3 0.0 all-to-all-done.got_ref
  56.3 0.1 adjoint.1
  56.4 16.9 %all_to_all.15.mine_ref = f32[16,2,8,512]{3,2,1,0:T(8,128)S(1)} all-to-all(f32[16,2,8,512]{3,2,1,0:T(8,128)S(1)} %adjoint.1), channel_id=1, replica_groups={{0,2,4,6,8,10,12,14,16,18,20,22,24,26,28,30},{1,3,5,7,9,11,13,15,17,19,..., dimensions={0} | all-to-all | bytes 1048576 | tf_op jit(solution)/shard_map/all_to_all | solution.py:469
  73.2 2.1 %collective-permute-start.3 = (f32[16,2,8,512]{3,2,1,0:T(8,128)S(1)}, f32[16,2,8,512]{3,2,1,0:T(8,128)S(1)}, u32[]{:S(2)}, u32[]{:S(2)}) collective-permute-start(f32[16,2,8,512]{3,2,1,0:T(8,128)S(1)} %all_to_all.15.mine_ref), channel_id=1, source_target_pairs={{0,1},{1,0},{2,3},{3,2},{4,5},{5,4},{6,7},{7,6},{8,9},{9,8},{10,11... | collective-permute-start | bytes 1572872 | tf_op jit(solution)/shard_map/ppermute | solution.py:489
  75.3 1.5 %collective-permute-done.3.other_ref = f32[16,2,8,512]{3,2,1,0:T(8,128)S(1)} collective-permute-done((f32[16,2,8,512]{3,2,1,0:T(8,128)S(1)}, f32[16,2,8,512]{3,2,1,0:T(8,128)S(1)}, u32[]{:S(2)}, u32[]{:S(2)}) %collective-permute-start.3) | collective-permute-done | bytes 524320 | tf_op jit(solution)/shard_map/ppermute | solution.py:489
  76.9 0.3 assemble.1
  77.1 1.3 %collective-permute-start.4 = (f32[8,32,512]{2,1,0:T(8,128)S(1)}, f32[8,32,512]{2,1,0:T(8,128)S(1)}, u32[]{:S(2)}, u32[]{:S(2)}) collective-permute-start(f32[8,32,512]{2,1,0:T(8,128)S(1)} %get-tuple-element.31), channel_id=1, source_target_pairs={{0,32},{32,64},{64,96},{1,33},{33,65},{65,97},{2,34},{34,66},{66,9... | collective-permute-start | bytes 1572872 | tf_op jit(solution)/shard_map/ppermute | solution.py:465
  78.4 1.5 %collective-permute-start.5 = (f32[8,32,512]{2,1,0:T(8,128)S(1)}, f32[8,32,512]{2,1,0:T(8,128)S(1)}, u32[]{:S(2)}, u32[]{:S(2)}) collective-permute-start(f32[8,32,512]{2,1,0:T(8,128)S(1)} %get-tuple-element.32), channel_id=1, source_target_pairs={{32,0},{64,32},{96,64},{33,1},{65,33},{97,65},{34,2},{66,34},{98,6... | collective-permute-start | bytes 1572872 | tf_op jit(solution)/shard_map/ppermute | solution.py:465
  79.9 0.0 copy-start.1
  79.9 9.4 %backward_own.1 = (f32[8,256,512]{2,1,0:T(8,128)}, f32[2,8,32,512]{3,2,1,0:T(8,128)S(1)}) custom-call(f32[8,256,512]{2,1,0:T(8,128)} %alpha_hbm.5, bf16[8,2,256,512]{3,2,1,0:T(8,128)(2,1)} %perts_hbm.5, f32[2,256,512]{2,1,0:T(8,128)S(1)} %bitcast.3, bf16[256,768]{1,0:T(8,128)(2,1)S(1)} %copy-done.5, bf16[2,1152,256]{2,1,0:T(8,128)(2,1)} %constant.8.clone.across_hbm.across_ref), custom_call_target="tpu_custom_call" | custom-call | flops 1000000 | tf_op jit(solution)/shard_map/backward_own/pallas_call | solution.py:355
  89.3 0.1 collective-permute-done.4.halo_ref
  89.5 1.6 %backward_edge.2.grad_hbm = f32[8,256,512]{2,1,0:T(8,128)} custom-call(f32[8,256,512]{2,1,0:T(8,128)} %get-tuple-element.29.grad_hbm, f32[2,8,32,512]{3,2,1,0:T(8,128)S(1)} %get-tuple-element.30.edge_ref, f32[8,32,512]{2,1,0:T(8,128)S(1)} %collective-permute-done.4.halo_ref, bf16[2,256,768]{2,1,0:T(8,128)(2,1)S(1)} %copy-done.2, ...), custom_call_target="tpu_custom_call", output_to_operand_aliasing={{}: (0, {})} | custom-call | flops 500000000 | bytes 3145728 | tf_op jit(solution)/shard_map/backward_edge/pallas_call | solution.py:383
  91.1 2.2 %collective-permute-done.5.halo_ref = f32[8,32,512]{2,1,0:T(8,128)S(1)} collective-permute-done((f32[8,32,512]{2,1,0:T(8,128)S(1)}, f32[8,32,512]{2,1,0:T(8,128)S(1)}, u32[]{:S(2)}, u32[]{:S(2)}) %collective-permute-start.5) | collective-permute-done | bytes 524320 | tf_op jit(solution)/shard_map/ppermute | solution.py:465
  93.3 1.6 %backward_edge.3 = f32[8,256,512]{2,1,0:T(8,128)} custom-call(f32[8,256,512]{2,1,0:T(8,128)} %backward_edge.2.grad_hbm, f32[2,8,32,512]{3,2,1,0:T(8,128)S(1)} %get-tuple-element.30.edge_ref, f32[8,32,512]{2,1,0:T(8,128)S(1)} %collective-permute-done.5.halo_ref, bf16[2,256,768]{2,1,0:T(8,128)(2,1)S(1)} %copy-done.2, ...), custom_call_target="tpu_custom_call", output_to_operand_aliasing={{}: (0, {})} | custom-call | flops 500000000 | bytes 3145728 | tf_op jit(solution)/shard_map/backward_edge/pallas_call | solution.py:383
  (9 shorter events, 0.0 us)
Async XLA Ops:
  0.0 22.0 %copy-start.5 = (bf16[256,768]{1,0:T(8,128)(2,1)S(1)}, bf16[256,768]{1,0:T(8,128)(2,1)}, u32[]{:S(2)}) copy-start(bf16[256,768]{1,0:T(8,128)(2,1)} %constant.6.clone.down_hbm) | copy-start | bytes 1179652
  3.6 26.9 %collective-permute-start = (f32[8,32,512]{2,1,0:T(8,128)}, f32[8,32,512]{2,1,0:T(8,128)}, u32[]{:S(2)}, u32[]{:S(2)}) collective-permute-start(f32[8,32,512]{2,1,0:T(8,128)} %get-tuple-element.19), channel_id=1, source_target_pairs={{0,32},{32,64},{64,96},{1,33},{33,65},{65,97},{2,34},{34,66},{66,9... | collective-permute-start | bytes 1572872 | tf_op jit(solution)/shard_map/ppermute | solution.py:465
  8.4 22.0 %collective-permute-start.1 = (f32[8,32,512]{2,1,0:T(8,128)}, f32[8,32,512]{2,1,0:T(8,128)}, u32[]{:S(2)}, u32[]{:S(2)}) collective-permute-start(f32[8,32,512]{2,1,0:T(8,128)} %get-tuple-element.20), channel_id=1, source_target_pairs={{32,0},{64,32},{96,64},{33,1},{65,33},{97,65},{34,2},{66,34},{98,6... | collective-permute-start | bytes 1572872 | tf_op jit(solution)/shard_map/ppermute | solution.py:465
  9.7 28.5 %all-to-all-start.1 = ((f32[128,2,768]{2,1,0:T(2,128)}), f32[128,2,768]{2,1,0:T(2,128)}, u32[]{:S(2)}, u32[]{:S(2)}) async-start(f32[128,2,768]{2,1,0:T(2,128)} %get-tuple-element.25), calls=%async_computation.1 | async-start | bytes 1572864 | tf_op jit(solution)/shard_map/all_to_all | solution.py:483
  22.0 8.5 %copy-start = (bf16[2,1152,256]{2,1,0:T(8,128)(2,1)S(1)}, bf16[2,1152,256]{2,1,0:T(8,128)(2,1)}, u32[]{:S(2)}) copy-start(bf16[2,1152,256]{2,1,0:T(8,128)(2,1)} %constant.8.clone.across_hbm.across_ref) | copy-start | bytes 3538948
  22.0 8.5 %copy-start.2 = (bf16[2,256,768]{2,1,0:T(8,128)(2,1)S(1)}, bf16[2,256,768]{2,1,0:T(8,128)(2,1)}, u32[]{:S(2)}) copy-start(bf16[2,256,768]{2,1,0:T(8,128)(2,1)} %constant.7.clone.down_ref) | copy-start | bytes 2359300
  22.0 8.5 %copy-start.3 = (bf16[8,2,32,512]{3,2,1,0:T(8,128)(2,1)S(1)}, bf16[8,2,32,512]{3,2,1,0:T(8,128)(2,1)}, u32[]{:S(2)}) copy-start(bf16[8,2,32,512]{3,2,1,0:T(8,128)(2,1)} %get-tuple-element.21.perts_first_ref) | copy-start | bytes 1572868
  22.0 8.5 %copy-start.4 = (bf16[8,2,32,512]{3,2,1,0:T(8,128)(2,1)S(1)}, bf16[8,2,32,512]{3,2,1,0:T(8,128)(2,1)}, u32[]{:S(2)}) copy-start(bf16[8,2,32,512]{3,2,1,0:T(8,128)(2,1)} %get-tuple-element.22.perts_last_ref) | copy-start | bytes 1572868
  33.1 2.7 %collective-permute-start.2 = (f32[16,2,8,512]{3,2,1,0:T(8,128)S(1)}, f32[16,2,8,512]{3,2,1,0:T(8,128)S(1)}, u32[]{:S(2)}, u32[]{:S(2)}) collective-permute-start(f32[16,2,8,512]{3,2,1,0:T(8,128)S(1)} %get-tuple-element.24), channel_id=1, source_target_pairs={{0,1},{1,0},{2,3},{3,2},{4,5},{5,4},{6,7},{7,6},{8,9},{9,8},{10,11... | collective-permute-start | bytes 1572872 | tf_op jit(solution)/shard_map/ppermute | solution.py:485
  38.2 18.1 %all-to-all-start = ((f32[16,2,8,512]{3,2,1,0:T(8,128)}), f32[16,2,8,512]{3,2,1,0:T(8,128)S(1)}, u32[]{:S(2)}, u32[]{:S(2)}) async-start(f32[16,2,8,512]{3,2,1,0:T(8,128)} %add.3), calls=%async_computation | async-start | bytes 1048576 | tf_op jit(solution)/shard_map/all_to_all | solution.py:469
  45.1 11.2 %copy-start.6 = (f32[2,8,512]{2,1,0:T(8,128)S(1)}, f32[2,8,512]{2,1,0:T(8,128)}, u32[]{:S(2)}) copy-start(f32[2,8,512]{2,1,0:T(8,128)} %back_ref.1) | copy-start | bytes 98308
  73.2 3.6 %collective-permute-start.3 = (f32[16,2,8,512]{3,2,1,0:T(8,128)S(1)}, f32[16,2,8,512]{3,2,1,0:T(8,128)S(1)}, u32[]{:S(2)}, u32[]{:S(2)}) collective-permute-start(f32[16,2,8,512]{3,2,1,0:T(8,128)S(1)} %all_to_all.15.mine_ref), channel_id=1, source_target_pairs={{0,1},{1,0},{2,3},{3,2},{4,5},{5,4},{6,7},{7,6},{8,9},{9,8},{10,11... | collective-permute-start | bytes 1572872 | tf_op jit(solution)/shard_map/ppermute | solution.py:489
  77.1 12.4 %collective-permute-start.4 = (f32[8,32,512]{2,1,0:T(8,128)S(1)}, f32[8,32,512]{2,1,0:T(8,128)S(1)}, u32[]{:S(2)}, u32[]{:S(2)}) collective-permute-start(f32[8,32,512]{2,1,0:T(8,128)S(1)} %get-tuple-element.31), channel_id=1, source_target_pairs={{0,32},{32,64},{64,96},{1,33},{33,65},{65,97},{2,34},{34,66},{66,9... | collective-permute-start | bytes 1572872 | tf_op jit(solution)/shard_map/ppermute | solution.py:465
  78.4 14.9 %collective-permute-start.5 = (f32[8,32,512]{2,1,0:T(8,128)S(1)}, f32[8,32,512]{2,1,0:T(8,128)S(1)}, u32[]{:S(2)}, u32[]{:S(2)}) collective-permute-start(f32[8,32,512]{2,1,0:T(8,128)S(1)} %get-tuple-element.32), channel_id=1, source_target_pairs={{32,0},{64,32},{96,64},{33,1},{65,33},{97,65},{34,2},{66,34},{98,6... | collective-permute-start | bytes 1572872 | tf_op jit(solution)/shard_map/ppermute | solution.py:465
  79.9 9.6 %copy-start.1 = (bf16[2,1152,256]{2,1,0:T(8,128)(2,1)S(1)}, bf16[2,1152,256]{2,1,0:T(8,128)(2,1)}, u32[]{:S(2)}) copy-start(bf16[2,1152,256]{2,1,0:T(8,128)(2,1)} %constant.8.clone.across_hbm.across_ref) | copy-start | bytes 3538948
